TPU v7x, 32 devices: a whole 2x2x4 slice. The times are simulated.
32 devices in a mesh: gx: 8 (over y, x, core), gy: 4 (over z).
Axes of the slice: x: 2, y: 2, z: 4, core: 2. Of those that a mesh axis runs over, the one named last changes fastest.
Arguments:
- node_latents: bfloat16 [8192, 128], P(('gx', 'gy')), may hold values from -6 to 6
- edge_latents: bfloat16 [8192, 64, 128], P(('gx', 'gy')), may hold values from -6 to 6
- node_cotangent: bfloat16 [8192, 128], P(('gx', 'gy')), may hold values from -6 to 6
- edge_cotangent: bfloat16 [8192, 64, 128], P(('gx', 'gy')), may hold values from -6 to 6
- neighbours: int32 [8192, 64], P(('gx', 'gy')), may hold values from 0 to 831, as said below
- edge_mask: int32 [8192, 64], P(('gx', 'gy')), may hold values from 0 to 1, as said below
- send_table: int32 [32, 64], P(('gx', 'gy')), may hold values from 0 to 255, as said below
- counts: int32 [32], P(('gx', 'gy')), may hold values from 85 to 256, as said below
- weights: float32 [9, 128, 128], replicated, may hold values from -0.375 to 0.375
- vectors: float32 [10, 128], replicated, may hold values from 0.1 to 1.9
- weights_m: float32 [9, 128, 128], replicated, may hold values from -0.010416667 to 0.010416667
- vectors_m: float32 [10, 128], replicated, may hold values from -0.041666668 to 0.041666668
- weights_v: float32 [9, 128, 128], replicated, may hold values from 6.781684e-06 to 2.7126736e-05
- vectors_v: float32 [10, 128], replicated, may hold values from 0.000108506945 to 0.00043402778
- weights_ema: float32 [9, 128, 128], replicated, may hold values from -0.375 to 0.375
- vectors_ema: float32 [10, 128], replicated, may hold values from 0.1 to 1.9
Outputs:
- nodes_out: bfloat16 [8192, 128], P(('gx', 'gy'))
- edges_out: bfloat16 [8192, 64, 128], P(('gx', 'gy'))
- nodes_grad: bfloat16 [8192, 128], P(('gx', 'gy'))
- edges_grad: bfloat16 [8192, 64, 128], P(('gx', 'gy'))
- grad_norm: float32 [], replicated
- weights_m_new: float32 [9, 128, 128], replicated
- vectors_m_new: float32 [10, 128], replicated
- weights_v_new: float32 [9, 128, 128], replicated
- vectors_v_new: float32 [10, 128], replicated
- weights_new: float32 [9, 128, 128], replicated
- vectors_new: float32 [10, 128], replicated
- weights_copy: bfloat16 [9, 128, 128], replicated
- vectors_copy: bfloat16 [10, 128], replicated
- weights_ema_new: float32 [9, 128, 128], replicated
- vectors_ema_new: float32 [10, 128], replicated
Inputs may be any that keep to these rules, and one draw needn't show every extreme that they name: `counts`: live particles of a device are its first rows; the last device is full. `edge_mask`: slot k of a particle is live when k is below its degree; each live particle has 1 to 60 live slots, dead particles none; some particle has 60. `neighbours`: a live slot names a live own row (0 to 255) or 256 + s * 64 + j, row j of halo slot s of a device inside the grid, never the centre slot s = 4; dead slots hold 0. `send_table`: distinct live rows of the device.
All inputs are finite; a program needn't handle non-finite values.
Results may differ from a plain program's by a relative error of at most 0.008.
Values may be sent and summed in bfloat16 or wider, within the bound.
No kernel may reach another device: no remote copies, remote signals or barrier semaphores. Data moves between devices by JAX's collectives and lax.ppermute only.
A program may use at most 128 MiB of HBM per device.

v0:
```python
import functools

import jax
import jax.numpy as jnp
from jax import lax
from jax.experimental import pallas as pl
from jax.experimental.pallas import tpu as pltpu
from jax.sharding import PartitionSpec as P

STEP = 10


first_decay = 0.5
second_decay = 0.5
adam_epsilon = 1e-08
weight_decay = 0.01
matrix_rate = 0.05
vector_rate = 0.2
average_decay = 0.9
clip_norm = 1.0
norm_epsilon = 1e-05


def neighbour_pairs(count):
    near = [(i, i ^ 1) for i in range(count) if (i ^ 1) < count]
    far = [(i, i + 1) for i in range(1, count - 1, 2)]
    return near, far + [(target, source) for source, target in far]


def extended(block, sides):
    for axis, dim in sides:
        near, far = neighbour_pairs(lax.axis_size(axis))
        from_far = lax.ppermute(block, axis, far)
        from_near = lax.ppermute(block, axis, near)
        even = lax.axis_index(axis) % 2 == 0
        low = jnp.where(even, from_far, from_near)
        high = jnp.where(even, from_near, from_far)
        block = jnp.concatenate([low, block, high], axis=dim)
    return block


def returned_along(parts, axis):
    near, far = neighbour_pairs(lax.axis_size(axis))
    even = lax.axis_index(axis) % 2 == 0
    low, high = parts[0].astype(jnp.bfloat16), parts[2].astype(jnp.bfloat16)
    from_far = lax.ppermute(jnp.where(even, low, high), axis, far)
    from_near = lax.ppermute(jnp.where(even, high, low), axis, near)
    return parts[1] + from_far.astype(jnp.float32) + from_near.astype(jnp.float32)


def stages(count):
    result, stride = [], 1
    while stride < count:
        factor = 2 if stride == 1 else min(4, count // stride)
        result.append((stride, factor))
        stride *= factor
    return result


def sum_everywhere(total):
    rows, width = total.shape
    split = stages(lax.axis_size("gx"))
    whole_rows = -(-rows // (16 * lax.axis_size("gx"))) * 16 * lax.axis_size("gx")
    total = jnp.pad(total, ((0, whole_rows - rows), (0, 0))).astype(jnp.bfloat16)
    index = lax.axis_index("gx")

    def partners(axis, stride, mask):
        return [(i, i ^ (mask * stride)) for i in range(lax.axis_size(axis))]

    for stride, factor in split:
        part = (index // stride) % factor
        height = total.shape[0] // factor
        mine = lax.dynamic_slice_in_dim(total, part * height, height, 0).astype(jnp.float32)
        for mask in range(factor - 1, 0, -1):
            piece = lax.dynamic_slice_in_dim(total, (part ^ mask) * height, height, 0)
            mine = mine + lax.ppermute(piece, "gx", partners("gx", stride, mask)).astype(jnp.float32)
        total = mine.astype(jnp.bfloat16)
    terms = [total.astype(jnp.float32)] + [
        lax.ppermute(total, "gy", partners("gy", 1, mask)).astype(jnp.float32)
        for mask in range(1, lax.axis_size("gy"))
    ]
    while len(terms) > 1:
        terms = [terms[i] + terms[i + 1] for i in range(0, len(terms), 2)]
    total = terms[0].astype(jnp.bfloat16)
    for stride, factor in reversed(split):
        part = (index // stride) % factor
        height = total.shape[0]
        joined = jnp.zeros((factor * height, width), jnp.bfloat16)
        joined = lax.dynamic_update_slice_in_dim(joined, total, part * height, 0)
        for mask in range(factor - 1, 0, -1):
            piece = lax.ppermute(total, "gx", partners("gx", stride, mask))
            joined = lax.dynamic_update_slice_in_dim(joined, piece, (part ^ mask) * height, 0)
        total = joined
    return total[:rows].astype(jnp.float32)


def selector(indices, width, dtype):
    columns = lax.broadcasted_iota(jnp.int32, (indices.shape[0], width), 1)
    return (indices[:, None] == columns).astype(dtype)


def adamw(param, grad, moment, second, average, scale, rate):
    clipped = grad * scale
    moment_new = first_decay * moment + (1.0 - first_decay) * clipped
    second_new = second_decay * second + (1.0 - second_decay) * clipped * clipped
    corrected = moment_new / (1.0 - first_decay**STEP)
    denom = jnp.sqrt(second_new / (1.0 - second_decay**STEP)) + adam_epsilon
    param_new = param - rate * (corrected / denom + weight_decay * param)
    average_new = average_decay * average + (1.0 - average_decay) * param_new
    return (moment_new, second_new, param_new, average_new)


CHUNK = 16
GROUP = 32
TILE = CHUNK * GROUP
LANES = 128
LOW_SCALE = 256.0


def dot(left, right):
    return jnp.dot(left, right, preferred_element_type=jnp.float32)


def dot_nt(left, right):
    return lax.dot_general(
        left, right, (((1,), (1,)), ((), ())), preferred_element_type=jnp.float32
    )


def dot_tn(left, right):
    return lax.dot_general(
        left, right, (((0,), (0,)), ((), ())), preferred_element_type=jnp.float32
    )


def split_pair(values):
    high = values.astype(jnp.bfloat16)
    low = ((values - high.astype(jnp.float32)) * LOW_SCALE).astype(jnp.bfloat16)
    return jnp.concatenate([high, low], axis=1)


def halves(pair):
    width = pair.shape[1] // 2
    return pair[:, :width] + pair[:, width:] * (1.0 / LOW_SCALE)


def silu_and_slope(values):
    gate = 0.5 * jnp.tanh(0.5 * values) + 0.5
    act = values * gate
    return act, gate + act * (1.0 - gate)


def row_mean(values):
    return jnp.mean(values, axis=-1, keepdims=True)


def normalized(values):
    center = values - row_mean(values)
    inverse = lax.rsqrt(row_mean(center * center) + norm_epsilon)
    return center * inverse, inverse


def normalized_back(upstream, unit, inverse):
    return inverse * (upstream - row_mean(upstream) - unit * row_mean(upstream * unit))


def column_total(values):
    return jnp.sum(values, axis=0, keepdims=True)


def layer_kernel(
    halo,
    count_ref,
    neighbour_ref,
    mask_ref,
    table_ref,
    upstream_ref,
    weights_ref,
    vectors_ref,
    edges_hbm,
    cotangent_hbm,
    nodes_out_ref,
    edges_out_hbm,
    edges_grad_hbm,
    node_part_ref,
    halo_grad_ref,
    grads_ref,
    edges_buf,
    cotangent_buf,
    kept_edges,
    kept_index,
    kept_act1,
    kept_act2,
    kept_slope1,
    kept_slope2,
    kept_unit,
    kept_inverse,
    low_ref,
    sender_ref,
    receiver_ref,
    neighbour_rows,
    segment_ref,
    chunk_sums,
    index_acc,
    mat_acc,
    vec_acc,
    work,
    upstream_tile,
    degree_rows,
    degree_smem,
    list_smem,
    in_sems,
    out_sems,
    degree_sem,
):
    f32, bf16 = jnp.float32, jnp.bfloat16
    particles, slots = neighbour_ref.shape
    per_particle = slots // CHUNK
    chunks = particles * per_particle
    rows, width = table_ref.shape
    index_width = index_acc.shape[1] - width
    pieces = in_sems.shape[0] // 2
    piece = chunks // pieces

    loads = []
    for order, (source, target) in enumerate(
        ((edges_hbm, edges_buf), (cotangent_hbm, cotangent_buf))
    ):
        loads.append(
            [
                pltpu.make_async_copy(
                    source.at[pl.ds(p * piece, piece)],
                    target.at[pl.ds(p * piece, piece)],
                    in_sems.at[order * pieces + p],
                )
                for p in range(pieces)
            ]
        )
    for copy in loads[0] + loads[1]:
        copy.start()
    edges_buf[chunks] = jnp.zeros((CHUNK, width), bf16)
    cotangent_buf[chunks] = jnp.zeros((CHUNK, width), bf16)

    mask = mask_ref[...].astype(f32)
    degree_rows[...] = jnp.zeros(degree_rows.shape, jnp.int32)
    degree_rows[:, 0:particles] = dot_nt(jnp.ones((8, slots), bf16), mask.astype(bf16)).astype(
        jnp.int32
    )
    fetch = pltpu.make_async_copy(degree_rows, degree_smem, degree_sem)
    fetch.start()

    neighbour = neighbour_ref[...]
    after_centre = particles + 5 * halo
    neighbour = jnp.where(neighbour >= after_centre, neighbour - halo, neighbour)
    neighbour_rows[...] = jnp.zeros(neighbour_rows.shape, f32)
    neighbour_rows[0:particles, 0:slots] = neighbour.astype(f32)

    for block in range(weights_ref.shape[0]):
        low_ref[block] = weights_ref[block].astype(bf16)
    vectors = vectors_ref[...]

    def vector(row):
        return vectors[row : row + 1, :]

    latents = table_ref[0:particles, :]
    sender_ref[...] = split_pair(dot(table_ref[...], low_ref[2]))
    receiver_ref[0:particles, :] = dot(latents, low_ref[1]) + vector(0)
    receiver_ref[particles:, :] = jnp.zeros((receiver_ref.shape[0] - particles, width), f32)

    degree = jnp.sum(mask, axis=1, keepdims=True).astype(jnp.int32)
    taken = jnp.broadcast_to(((degree + (CHUNK - 1)) >> 4).astype(f32), (particles, width))
    before = lax.broadcasted_iota(jnp.int32, (particles, particles), 1) < lax.broadcasted_iota(
        jnp.int32, (particles, particles), 0
    )
    begin = dot(before.astype(bf16), taken.astype(bf16))
    end = begin + taken
    for block in range(chunks // width):
        lane = lax.broadcasted_iota(jnp.int32, (particles, width), 1).astype(f32) + block * width
        segment_ref[:, block * width : (block + 1) * width] = (
            (lane >= begin) & (lane < end)
        ).astype(bf16)
    chunk_sums[...] = jnp.zeros(chunk_sums.shape, f32)
    index_acc[...] = jnp.zeros(index_acc.shape, f32)
    mat_acc[...] = jnp.zeros(mat_acc.shape, f32)
    vec_acc[...] = jnp.zeros(vec_acc.shape, f32)

    fetch.wait()

    def list_particle(i, position):
        used = (degree_smem[0, i] + (CHUNK - 1)) >> 4
        for c in range(per_particle):
            list_smem[position + c] = i * per_particle + c
        return position + used

    total = lax.fori_loop(0, particles, list_particle, jnp.int32(0), unroll=8)
    for j in range(GROUP):
        list_smem[total + j] = chunks
    tiles = (total + (GROUP - 1)) // GROUP

    for copy in loads[0]:
        copy.wait()

    sublane = lax.broadcasted_iota(jnp.int32, (CHUNK, width), 0)
    diagonal = lax.broadcasted_iota(jnp.int32, (CHUNK, width), 1) - sublane

    def entry(t, j):
        chunk = list_smem[t * GROUP + j]
        particle = chunk // per_particle
        first = (chunk % per_particle) * CHUNK
        live = (sublane < degree_smem[0, particle] - first).astype(f32)
        return chunk, particle, first, live

    def flat(ref, t):
        return ref[pl.ds(t * GROUP, GROUP)].reshape(TILE, width)

    def one_hot(t):
        index = flat(kept_index, t)
        lane = lax.broadcasted_iota(jnp.int32, (TILE, width), 1)
        return [(index == lane + b * width).astype(bf16) for b in range(index_width // width)]

    def forward(t, carry):
        base = t * GROUP
        entries = [entry(t, j) for j in range(GROUP)]
        for j, (chunk, particle, first, live) in enumerate(entries):
            kept_edges[base + j] = edges_buf[chunk]
            row = jnp.broadcast_to(neighbour_rows[pl.ds(particle, 1), :], (CHUNK, width))
            index = jnp.sum(jnp.where(diagonal == first, row, 0.0), axis=1, keepdims=True)
            kept_index[base + j] = jnp.broadcast_to(index, (CHUNK, width)).astype(jnp.int32)
        edge_tile = flat(kept_edges, t)
        receiver = jnp.concatenate(
            [
                jnp.broadcast_to(receiver_ref[pl.ds(particle, 1), :], (CHUNK, width))
                for _, particle, _, _ in entries
            ],
            axis=0,
        )
        first_in = halves(dot(jnp.concatenate(one_hot(t), axis=1), sender_ref[...]))
        first_in = first_in + (dot(edge_tile, low_ref[0]) + receiver)
        act, slope = silu_and_slope(first_in)
        act = act.astype(bf16)
        kept_act1[pl.ds(base, GROUP)] = act.reshape(GROUP, CHUNK, width)
        kept_slope1[pl.ds(base, GROUP)] = slope.astype(bf16).reshape(GROUP, CHUNK, width)
        act, slope = silu_and_slope(dot(act, low_ref[3]) + vector(1))
        act = act.astype(bf16)
        kept_act2[pl.ds(base, GROUP)] = act.reshape(GROUP, CHUNK, width)
        kept_slope2[pl.ds(base, GROUP)] = slope.astype(bf16).reshape(GROUP, CHUNK, width)
        unit, inverse = normalized(dot(act, low_ref[4]) + vector(2))
        kept_unit[pl.ds(base, GROUP)] = unit.astype(bf16).reshape(GROUP, CHUNK, width)
        kept_inverse[pl.ds(base, GROUP)] = jnp.broadcast_to(inverse, (TILE, width)).reshape(
            GROUP, CHUNK, width
        )
        live = jnp.concatenate([item[3] for item in entries], axis=0)
        edges_new = edge_tile.astype(f32) + live * (unit * vector(3) + vector(4))
        chunk_sums[pl.ds(base, GROUP), :] = jnp.sum(
            (live * edges_new).reshape(GROUP, CHUNK, width), axis=1
        )
        edges_new = edges_new.astype(bf16).reshape(GROUP, CHUNK, width)
        for j, (chunk, _, _, _) in enumerate(entries):
            edges_buf[chunk] = edges_new[j]
        return carry

    lax.fori_loop(0, tiles, forward, 0)

    stores = [
        pltpu.make_async_copy(
            edges_buf.at[pl.ds(p * piece, piece)],
            edges_out_hbm.at[pl.ds(p * piece, piece)],
            out_sems.at[p],
        )
        for p in range(pieces)
    ]
    for copy in stores:
        copy.start()

    def segment_sum():
        return halves(dot(segment_ref[...], split_pair(chunk_sums[...])))

    aggregate = segment_sum().astype(bf16)
    act1, slope1 = silu_and_slope(
        dot(latents, low_ref[5]) + dot(aggregate, low_ref[6]) + vector(5)
    )
    act1 = act1.astype(bf16)
    act2, slope2 = silu_and_slope(dot(act1, low_ref[7]) + vector(6))
    act2 = act2.astype(bf16)
    unit, inverse = normalized(dot(act2, low_ref[8]) + vector(7))
    alive = (
        lax.broadcasted_iota(jnp.int32, (particles, width), 0) < count_ref[0]
    ).astype(f32)
    upstream = upstream_ref[...].astype(f32)
    nodes_out_ref[...] = (
        latents.astype(f32) + alive * (unit * vector(8) + vector(9))
    ).astype(bf16)
    held = alive * upstream
    third = normalized_back(held * vector(8), unit, inverse).astype(bf16)
    second = (slope2 * dot_nt(third, low_ref[8])).astype(bf16)
    first = (slope1 * dot_nt(second, low_ref[7])).astype(bf16)
    receiver_ref[0:particles, :] = dot_nt(first, low_ref[6])
    node_part_ref[...] = upstream + dot_nt(first, low_ref[5])

    def put_block(block, values):
        grads_ref[block * width : (block + 1) * width, :] = values

    put_block(5, dot_tn(latents, first))
    put_block(6, dot_tn(aggregate, first))
    put_block(7, dot_tn(act1, second))
    put_block(8, dot_tn(act2, third))
    tail = weights_ref.shape[0] * width
    grads_ref[tail:, :] = jnp.zeros((grads_ref.shape[0] - tail, width), f32)
    for row, values in enumerate(
        (first.astype(f32), second.astype(f32), third.astype(f32), held * unit, held)
    ):
        grads_ref[tail + 5 + row : tail + 6 + row, :] = column_total(values)

    for copy in loads[1]:
        copy.wait()

    def backward(t, carry):
        base = t * GROUP
        entries = [entry(t, j) for j in range(GROUP)]
        live = jnp.concatenate([item[3] for item in entries], axis=0)
        passed = jnp.concatenate(
            [
                cotangent_buf[chunk].astype(f32) + alive_rows * receiver_ref[pl.ds(particle, 1), :]
                for chunk, particle, _, alive_rows in entries
            ],
            axis=0,
        )
        upstream_tile[...] = passed
        held = live * passed
        unit = flat(kept_unit, t).astype(f32)
        third = normalized_back(held * vector(3), unit, flat(kept_inverse, t)).astype(bf16)
        second = (flat(kept_slope2, t).astype(f32) * dot_nt(third, low_ref[4])).astype(bf16)
        first = (flat(kept_slope1, t).astype(f32) * dot_nt(second, low_ref[3])).astype(bf16)
        result = (upstream_tile[...] + dot_nt(first, low_ref[0])).astype(bf16)
        result = result.reshape(GROUP, CHUNK, width)
        for j, (chunk, _, _, _) in enumerate(entries):
            cotangent_buf[chunk] = result[j]
        index_acc[...] += dot_tn(first, jnp.concatenate(one_hot(t) + [flat(kept_edges, t)], axis=1))
        mat_acc[0] += dot_tn(flat(kept_act1, t), second)
        mat_acc[1] += dot_tn(flat(kept_act2, t), third)
        first = first.astype(f32)
        chunk_sums[pl.ds(base, GROUP), :] = jnp.sum(first.reshape(GROUP, CHUNK, width), axis=1)
        for row, values in enumerate(
            (first, second.astype(f32), third.astype(f32), held * unit, held)
        ):
            vec_acc[8 * row : 8 * row + 8, :] += jnp.sum(
                values.reshape(TILE // 8, 8, width), axis=0
            )
        return carry

    lax.fori_loop(0, tiles, backward, 0)

    results = [
        pltpu.make_async_copy(
            cotangent_buf.at[pl.ds(p * piece, piece)],
            edges_grad_hbm.at[pl.ds(p * piece, piece)],
            out_sems.at[pieces + p],
        )
        for p in range(pieces)
    ]
    for copy in results:
        copy.start()

    receiver_grad = segment_sum().astype(bf16)
    sent = index_acc[:, 0:index_width].astype(bf16)
    put_block(0, index_acc[:, index_width:].T)
    put_block(1, dot_tn(latents, receiver_grad))
    put_block(2, dot(sent, table_ref[...]).T)
    put_block(3, mat_acc[0])
    put_block(4, mat_acc[1])
    table_grad = lax.dot_general(
        sent, low_ref[2], (((0,), (1,)), ((), ())), preferred_element_type=f32
    )
    node_part_ref[...] += dot_nt(receiver_grad, low_ref[1]) + table_grad[0:particles, :]
    halo_grad_ref[...] = table_grad[particles:, :].astype(bf16)
    for row in range(5):
        grads_ref[tail + row : tail + row + 1, :] = column_total(vec_acc[8 * row : 8 * row + 8, :])

    for copy in stores + results:
        copy.wait()


def layer_call(
    table, halo, counts, neighbours, edge_mask, upstream, weights, vectors, edges, cotangents
):
    f32, bf16, i32 = jnp.float32, jnp.bfloat16, jnp.int32
    particles, slots = neighbours.shape
    width = table.shape[1]
    table_rows = table.shape[0]
    chunks = particles * slots // CHUNK
    pieces = 4
    grad_rows = weights.shape[0] * width + 16
    whole = pl.BlockSpec(memory_space=pltpu.VMEM)
    outside = pl.BlockSpec(memory_space=pl.ANY)
    edge_shape = (chunks, CHUNK, width)
    kept = pltpu.VMEM(edge_shape, bf16)
    buffer = pltpu.VMEM((chunks + 1, CHUNK, width), bf16)
    return pl.pallas_call(
        functools.partial(layer_kernel, halo),
        out_shape=(
            jax.ShapeDtypeStruct((particles, width), bf16),
            jax.ShapeDtypeStruct(edge_shape, bf16),
            jax.ShapeDtypeStruct(edge_shape, bf16),
            jax.ShapeDtypeStruct((particles, width), f32),
            jax.ShapeDtypeStruct((table_rows - particles, width), bf16),
            jax.ShapeDtypeStruct((grad_rows, width), f32),
        ),
        in_specs=[
            pl.BlockSpec(memory_space=pltpu.SMEM),
            whole,
            whole,
            whole,
            whole,
            whole,
            whole,
            outside,
            outside,
        ],
        out_specs=(whole, outside, outside, whole, whole, whole),
        scratch_shapes=[
            buffer,
            buffer,
            kept,
            pltpu.VMEM(edge_shape, i32),
            kept,
            kept,
            kept,
            kept,
            kept,
            pltpu.VMEM(edge_shape, f32),
            pltpu.VMEM(weights.shape, bf16),
            pltpu.VMEM((table_rows, 2 * width), bf16),
            pltpu.VMEM((particles + 8, width), f32),
            pltpu.VMEM((particles + 8, width), f32),
            pltpu.VMEM((particles, chunks), bf16),
            pltpu.VMEM((chunks, width), f32),
            pltpu.VMEM((width, table_rows + width), f32),
            pltpu.VMEM((2, width, width), f32),
            pltpu.VMEM((40, width), f32),
            pltpu.VMEM((TILE, width), f32),
            pltpu.VMEM((TILE, width), f32),
            pltpu.VMEM((8, particles + LANES), i32),
            pltpu.SMEM((8, particles + LANES), i32),
            pltpu.SMEM((chunks + GROUP + 16,), i32),
            pltpu.SemaphoreType.DMA((2 * pieces,)),
            pltpu.SemaphoreType.DMA((2 * pieces,)),
            pltpu.SemaphoreType.DMA,
        ],
        compiler_params=pltpu.CompilerParams(vmem_limit_bytes=60 * 1024 * 1024),
        name="edge_layer",
    )(
        counts,
        neighbours,
        edge_mask,
        table,
        upstream,
        weights,
        vectors,
        edges.reshape(edge_shape),
        cotangents.reshape(edge_shape),
    )


def per_device(
    node_latents,
    edge_latents,
    node_cotangent,
    edge_cotangent,
    neighbours,
    edge_mask,
    send_table,
    counts,
    weights,
    vectors,
    weights_m,
    vectors_m,
    weights_v,
    vectors_v,
    weights_ema,
    vectors_ema,
):
    tok_rows, width = node_latents.shape
    halo = send_table.shape[1]
    boundary_pick = selector(send_table[0], tok_rows, jnp.bfloat16)
    boundary = jnp.dot(boundary_pick, node_latents, preferred_element_type=jnp.float32)
    halo_grid = extended(boundary.astype(jnp.bfloat16)[None, None], (("gx", 0), ("gy", 1)))
    halo_rows = halo_grid.reshape(9, halo, width)
    node_table = jnp.concatenate(
        [
            node_latents,
            halo_rows[:4].reshape(-1, width),
            halo_rows[5:].reshape(-1, width),
        ],
        axis=0,
    )
    nodes_out, edges_out, edges_in_grad, node_part, halo_grad, partial = layer_call(
        node_table,
        halo,
        counts,
        neighbours,
        edge_mask,
        node_cotangent,
        weights,
        vectors,
        edge_latents,
        edge_cotangent,
    )
    halo_grad = halo_grad.astype(jnp.float32)
    halo_grad = jnp.concatenate(
        [halo_grad[: 4 * halo], jnp.zeros((halo, width), jnp.float32), halo_grad[4 * halo :]]
    ).reshape(3, 3, halo, width)
    boundary_grad = returned_along(returned_along(halo_grad, "gx"), "gy")
    returned = lax.dot_general(
        boundary_pick.astype(jnp.float32),
        boundary_grad,
        (((0,), (0,)), ((), ())),
        precision=lax.Precision.HIGHEST,
        preferred_element_type=jnp.float32,
    )
    nodes_in_grad = node_part + returned
    summed = sum_everywhere(partial)
    mat_rows = weights.shape[0] * weights.shape[1]
    vec_rows = vectors.shape[0]
    grad_mats = summed[:mat_rows].reshape(weights.shape)
    grad_vecs = summed[mat_rows : mat_rows + vec_rows]
    grad_norm = jnp.sqrt(jnp.sum(grad_mats * grad_mats) + jnp.sum(grad_vecs * grad_vecs))
    scale = clip_norm / jnp.maximum(grad_norm, clip_norm)
    weights_m_new, weights_v_new, weights_new, weights_ema_new = adamw(
        weights, grad_mats, weights_m, weights_v, weights_ema, scale, matrix_rate
    )
    vectors_m_new, vectors_v_new, vectors_new, vectors_ema_new = adamw(
        vectors, grad_vecs, vectors_m, vectors_v, vectors_ema, scale, vector_rate
    )
    return (
        nodes_out,
        edges_out.reshape(edge_latents.shape),
        nodes_in_grad.astype(jnp.bfloat16),
        edges_in_grad.reshape(edge_latents.shape),
        grad_norm,
        weights_m_new,
        vectors_m_new,
        weights_v_new,
        vectors_v_new,
        weights_new,
        vectors_new,
        weights_new.astype(jnp.bfloat16),
        vectors_new.astype(jnp.bfloat16),
        weights_ema_new,
        vectors_ema_new,
    )


def solution(mesh):
    in_specs = (
        P(("gx", "gy"), None),
        P(("gx", "gy"), None, None),
        P(("gx", "gy"), None),
        P(("gx", "gy"), None, None),
        P(("gx", "gy"), None),
        P(("gx", "gy"), None),
        P(("gx", "gy"), None),
        P(("gx", "gy")),
        P(),
        P(),
        P(),
        P(),
        P(),
        P(),
        P(),
        P(),
    )
    out_specs = (
        P(("gx", "gy"), None),
        P(("gx", "gy"), None, None),
        P(("gx", "gy"), None),
        P(("gx", "gy"), None, None),
        P(),
        P(),
        P(),
        P(),
        P(),
        P(),
        P(),
        P(),
        P(),
        P(),
        P(),
    )
    return jax.shard_map(
        per_device, mesh=mesh, in_specs=in_specs, out_specs=out_specs, check_vma=False
    )
```

profile of v0, /device:TPU:0, one launch (start us, length us, event | category | flops | bytes accessed | tf_op | source)
XLA Modules:
  0.0 101.4 jit_solution(16963129887810329705)
XLA Ops:
  0.6 1.0 %fusion.1 = bf16[1,1,64,128]{3,2,1,0:T(8,128)(2,1)S(1)} fusion(bf16[256,128]{1,0:T(8,128)(2,1)} %param.16, s32[64]{0:T(128)} %bitcast.35), kind=kOutput, calls=%fused_computation.3 | convolution fusion | flops 4218880 | bytes 82176 | tf_op jit(solution)/shard_map/dot_general | solution.py:585
  3.1 3.0 %collective-permute-start.3 = (bf16[3,1,64,128]{3,2,1,0:T(8,128)(2,1)S(1)}, bf16[3,1,64,128]{3,2,1,0:T(8,128)(2,1)S(1)}, u32[]{:S(2)}, u32[]{:S(2)}) collective-permute-start(bf16[3,1,64,128]{3,2,1,0:T(8,128)(2,1)S(1)} %pad_maximum_fusion.4), channel_id=1, source_target_pairs={{0,1},{1,0},{2,3},{3,2},{4,5},{5,4},{6,7},{7,6},{8,9},{9,8},{10,11... | collective-permute-start | bytes 147464 | tf_op jit(solution)/shard_map/ppermute | solution.py:34
  7.5 1.6 %copy.31.neighbour_ref = s32[256,64]{1,0:T(8,128)} copy(s32[256,64]{0,1:T(8,128)} %param.20) | data formatting | bytes 131072 | tf_op args[4]
  9.1 1.6 %copy.32.mask_ref = s32[256,64]{1,0:T(8,128)} copy(s32[256,64]{0,1:T(8,128)} %param.21) | data formatting | bytes 131072 | tf_op args[5]
  10.7 1.5 %pad_maximum_fusion.table_ref = bf16[768,128]{1,0:T(8,128)(2,1)} fusion(bf16[256,128]{1,0:T(8,128)(2,1)S(1)} %bitcast.32, bf16[256,128]{1,0:T(8,128)(2,1)S(1)} %bitcast.31, bf16[256,128]{1,0:T(8,128)(2,1)} %param.16), kind=kLoop, calls=%fused_computation.15 | loop fusion | flops 589824 | bytes 393216 | tf_op jit(solution)/shard_map/concatenate | solution.py:588
  12.3 20.9 %edge_layer.1 = (bf16[256,128]{1,0:T(8,128)(2,1)}, bf16[1024,16,128]{2,1,0:T(8,128)(2,1)}, bf16[1024,16,128]{2,1,0:T(8,128)(2,1)}, f32[256,128]{1,0:T(8,128)}, b...) custom-call(s32[1]{0:T(128)S(6)} %copy.39.count_ref, s32[256,64]{1,0:T(8,128)} %copy.31.neighbour_ref, ...), custom_call_target="tpu_custom_call" | custom-call | tf_op jit(solution)/shard_map/edge_layer/pallas_call | solution.py:498
  34.1 4.1 %collective-permute-start.5 = (bf16[3,64,128]{2,1,0:T(8,128)(2,1)S(1)}, bf16[3,64,128]{2,1,0:T(8,128)(2,1)S(1)}, u32[]{:S(2)}, u32[]{:S(2)}) collective-permute-start(bf16[3,64,128]{2,1,0:T(8,128)(2,1)S(1)} %bitcast.34), channel_id=1, source_target_pairs={{0,4},{4,0},{8,12},{12,8},{16,20},{20,16},{24,28},{28,24},{1,5},{5... | collective-permute-start | bytes 147464 | tf_op jit(solution)/shard_map/ppermute | solution.py:47
  39.0 1.2 %convert.11 = bf16[1168,128]{1,0:T(8,128)(2,1)S(1)} convert(f32[1168,128]{1,0:T(8,128)} %get-tuple-element.26) | non-fusion elementwise | flops 149504 | bytes 897024 | tf_op jit(solution)/shard_map/convert
  40.3 4.8 %collective-permute-start.8 = (bf16[640,128]{1,0:T(8,128)(2,1)S(1)}, bf16[640,128]{1,0:T(8,128)(2,1)S(1)}, u32[]{:S(2)}, u32[]{:S(2)}) collective-permute-start(bf16[640,128]{1,0:T(8,128)(2,1)S(1)} %pad_dynamic-slice_fusion), channel_id=1, source_target_pairs={{0,4},{4,0},{8,12},{12,8},{16,20},{20,16},{24,28},{28,24},{1,5},{5... | collective-permute-start | bytes 491528 | tf_op jit(solution)/shard_map/ppermute | solution.py:76
  46.2 1.9 %collective-permute-start.9 = (bf16[160,128]{1,0:T(8,128)(2,1)S(1)}, bf16[160,128]{1,0:T(8,128)(2,1)S(1)}, u32[]{:S(2)}, u32[]{:S(2)}) collective-permute-start(bf16[160,128]{1,0:T(8,128)(2,1)S(1)} %get-tuple-element.39), channel_id=1, source_target_pairs={{0,24},{4,28},{8,16},{12,20},{16,8},{20,12},{24,0},{28,4},{1,25},{... | collective-permute-start | bytes 122888 | tf_op jit(solution)/shard_map/ppermute | solution.py:76
  48.2 1.4 %collective-permute-start.11 = (bf16[160,128]{1,0:T(8,128)(2,1)S(1)}, bf16[160,128]{1,0:T(8,128)(2,1)S(1)}, u32[]{:S(2)}, u32[]{:S(2)}) collective-permute-start(bf16[160,128]{1,0:T(8,128)(2,1)S(1)} %get-tuple-element.40), channel_id=1, source_target_pairs={{0,8},{4,12},{8,0},{12,4},{16,24},{20,28},{24,16},{28,20},{1,9},{5... | collective-permute-start | bytes 122888 | tf_op jit(solution)/shard_map/ppermute | solution.py:76
  49.9 1.3 %collective-permute-done.9 = bf16[160,128]{1,0:T(8,128)(2,1)S(1)} collective-permute-done((bf16[160,128]{1,0:T(8,128)(2,1)S(1)}, bf16[160,128]{1,0:T(8,128)(2,1)S(1)}, u32[]{:S(2)}, u32[]{:S(2)}) %collective-permute-start.9) | collective-permute-done | bytes 40992 | tf_op jit(solution)/shard_map/ppermute | solution.py:76
  51.2 0.9 collective-permute-done.11
  52.2 1.4 %collective-permute-done.10 = bf16[160,128]{1,0:T(8,128)(2,1)S(1)} collective-permute-done((bf16[160,128]{1,0:T(8,128)(2,1)S(1)}, bf16[160,128]{1,0:T(8,128)(2,1)S(1)}, u32[]{:S(2)}, u32[]{:S(2)}) %collective-permute-start.10) | collective-permute-done | bytes 40992 | tf_op jit(solution)/shard_map/ppermute | solution.py:76
  53.6 21.6 %collective-permute-start.14 = (bf16[160,128]{1,0:T(8,128)(2,1)S(1)}, bf16[160,128]{1,0:T(8,128)(2,1)S(1)}, u32[]{:S(2)}, u32[]{:S(2)}) collective-permute-start(bf16[160,128]{1,0:T(8,128)(2,1)S(1)} %add_convert_fusion.2), channel_id=1, source_target_pairs={{0,3},{1,2},{2,1},{3,0},{4,7},{5,6},{6,5},{7,4},{8,11},{9,10},{10,... | collective-permute-start | bytes 122888 | tf_op jit(solution)/shard_map/ppermute | solution.py:79
  75.2 2.7 %collective-permute-start.13 = (bf16[160,128]{1,0:T(8,128)(2,1)S(1)}, bf16[160,128]{1,0:T(8,128)(2,1)S(1)}, u32[]{:S(2)}, u32[]{:S(2)}) collective-permute-start(bf16[160,128]{1,0:T(8,128)(2,1)S(1)} %add_convert_fusion.2), channel_id=1, source_target_pairs={{0,2},{1,3},{2,0},{3,1},{4,6},{5,7},{6,4},{7,5},{8,10},{9,11},{10,... | collective-permute-start | bytes 122888 | tf_op jit(solution)/shard_map/ppermute | solution.py:79
  78.5 2.2 %collective-permute-done.13 = bf16[160,128]{1,0:T(8,128)(2,1)S(1)} collective-permute-done((bf16[160,128]{1,0:T(8,128)(2,1)S(1)}, bf16[160,128]{1,0:T(8,128)(2,1)S(1)}, u32[]{:S(2)}, u32[]{:S(2)}) %collective-permute-start.13) | collective-permute-done | bytes 40992 | tf_op jit(solution)/shard_map/ppermute | solution.py:79
  80.7 1.2 %collective-permute-done.12 = bf16[160,128]{1,0:T(8,128)(2,1)S(1)} collective-permute-done((bf16[160,128]{1,0:T(8,128)(2,1)S(1)}, bf16[160,128]{1,0:T(8,128)(2,1)S(1)}, u32[]{:S(2)}, u32[]{:S(2)}) %collective-permute-start.12) | collective-permute-done | bytes 40992 | tf_op jit(solution)/shard_map/ppermute | solution.py:79
  82.8 3.7 %collective-permute-start.7 = (bf16[64,128]{1,0:T(8,128)(2,1)S(1)}, bf16[64,128]{1,0:T(8,128)(2,1)S(1)}, u32[]{:S(2)}, u32[]{:S(2)}) collective-permute-start(bf16[64,128]{1,0:T(8,128)(2,1)S(1)} %get-tuple-element.51), channel_id=1, source_target_pairs={{0,1},{1,0},{2,3},{3,2},{4,5},{5,4},{6,7},{7,6},{8,9},{9,8},{10,11... | collective-permute-start | bytes 49160 | tf_op jit(solution)/shard_map/ppermute | solution.py:47
  86.5 1.6 %collective-permute-start.16 = (bf16[160,128]{1,0:T(8,128)(2,1)S(1)}, bf16[160,128]{1,0:T(8,128)(2,1)S(1)}, u32[]{:S(2)}, u32[]{:S(2)}) collective-permute-start(bf16[160,128]{1,0:T(8,128)(2,1)S(1)} %get-tuple-element.36), channel_id=1, source_target_pairs={{0,16},{4,20},{8,24},{12,28},{16,0},{20,4},{24,8},{28,12},{1,17},{... | collective-permute-start | bytes 122888 | tf_op jit(solution)/shard_map/ppermute | solution.py:91
  88.2 1.8 %collective-permute-start.17 = (bf16[160,128]{1,0:T(8,128)(2,1)S(1)}, bf16[160,128]{1,0:T(8,128)(2,1)S(1)}, u32[]{:S(2)}, u32[]{:S(2)}) collective-permute-start(bf16[160,128]{1,0:T(8,128)(2,1)S(1)} %get-tuple-element.36), channel_id=1, source_target_pairs={{0,8},{4,12},{8,0},{12,4},{16,24},{20,28},{24,16},{28,20},{1,9},{5... | collective-permute-start | bytes 122888 | tf_op jit(solution)/shard_map/ppermute | solution.py:91
  90.5 1.6 %collective-permute-done.17 = bf16[160,128]{1,0:T(8,128)(2,1)S(1)} collective-permute-done((bf16[160,128]{1,0:T(8,128)(2,1)S(1)}, bf16[160,128]{1,0:T(8,128)(2,1)S(1)}, u32[]{:S(2)}, u32[]{:S(2)}) %collective-permute-start.17) | collective-permute-done | bytes 40992 | tf_op jit(solution)/shard_map/ppermute | solution.py:91
  92.3 1.0 fusion
  97.8 1.6 %multiply_add_fusion.1 = (f32[9,128,128]{2,1,0:T(8,128)}, f32[9,128,128]{2,1,0:T(8,128)S(1)}, f32[9,128,128]{2,1,0:T(8,128)}, f32[9,128,128]{2,1,0:T(8,128)}) fusion(f32[9,128,128]{2,1,0:T(8,128)S(1)} %copy-done.2, f32[9,128,128]{2,1,0:T(8,128)S(1)} %copy-done, f32[9,128,128]{2,1,0:T(8,128)S(1)} %bitcast.28, f32[9,128,128]{2,1,0:T(8,128)S(1)} %copy-done.3, ...), kind=kLoop, calls=%fused_computation.7 | loop fusion | flops 2506752 | bytes 5308416 | tf_op jit(solution)/shard_map/add | solution.py:109
  (77 shorter events, 11.2 us)
Async XLA Ops:
  1.7 1.4 %collective-permute-start.1 = (bf16[1,1,64,128]{3,2,1,0:T(8,128)(2,1)S(1)}, bf16[1,1,64,128]{3,2,1,0:T(8,128)(2,1)S(1)}, u32[]{:S(2)}, u32[]{:S(2)}) collective-permute-start(bf16[1,1,64,128]{3,2,1,0:T(8,128)(2,1)S(1)} %fusion.1), channel_id=1, source_target_pairs={{0,4},{4,0},{8,12},{12,8},{16,20},{20,16},{24,28},{28,24},{1,5},{5... | collective-permute-start | bytes 49160 | tf_op jit(solution)/shard_map/ppermute | solution.py:34
  2.2 0.8 collective-permute-start
  3.1 7.6 %collective-permute-start.3 = (bf16[3,1,64,128]{3,2,1,0:T(8,128)(2,1)S(1)}, bf16[3,1,64,128]{3,2,1,0:T(8,128)(2,1)S(1)}, u32[]{:S(2)}, u32[]{:S(2)}) collective-permute-start(bf16[3,1,64,128]{3,2,1,0:T(8,128)(2,1)S(1)} %pad_maximum_fusion.4), channel_id=1, source_target_pairs={{0,1},{1,0},{2,3},{3,2},{4,5},{5,4},{6,7},{7,6},{8,9},{9,8},{10,11... | collective-permute-start | bytes 147464 | tf_op jit(solution)/shard_map/ppermute | solution.py:34
  6.1 4.6 %collective-permute-start.2 = (bf16[3,1,64,128]{3,2,1,0:T(8,128)(2,1)S(1)}, bf16[3,1,64,128]{3,2,1,0:T(8,128)(2,1)S(1)}, u32[]{:S(2)}, u32[]{:S(2)}) collective-permute-start(bf16[3,1,64,128]{3,2,1,0:T(8,128)(2,1)S(1)} %pad_maximum_fusion.4), channel_id=1, source_target_pairs={{1,2},{2,1},{5,6},{6,5},{9,10},{10,9},{13,14},{14,13},{17,18},{18,... | collective-permute-start | bytes 147464 | tf_op jit(solution)/shard_map/ppermute | solution.py:33
  33.2 59.1 %copy-start.5 = (f32[256,128]{1,0:T(8,128)S(1)}, f32[256,128]{1,0:T(8,128)}, u32[]{:S(2)}) copy-start(f32[256,128]{1,0:T(8,128)} %get-tuple-element.23) | copy-start | bytes 393220
  34.1 62.4 %copy-start.7 = (f32[10,128]{1,0:T(8,128)S(1)}, f32[10,128]{1,0:T(8,128)}, u32[]{:S(2)}) copy-start(f32[10,128]{1,0:T(8,128)} %vectors_ref.1) | copy-start | bytes 15364
  34.1 62.4 %copy-start.8 = (f32[10,128]{1,0:T(8,128)S(1)}, f32[10,128]{1,0:T(8,128)}, u32[]{:S(2)}) copy-start(f32[10,128]{1,0:T(8,128)} %param.31) | copy-start | bytes 15364
  34.1 62.4 %copy-start.9 = (f32[10,128]{1,0:T(8,128)S(1)}, f32[10,128]{1,0:T(8,128)}, u32[]{:S(2)}) copy-start(f32[10,128]{1,0:T(8,128)} %param.29) | copy-start | bytes 15364
  34.1 62.4 %copy-start.10 = (f32[10,128]{1,0:T(8,128)S(1)}, f32[10,128]{1,0:T(8,128)}, u32[]{:S(2)}) copy-start(f32[10,128]{1,0:T(8,128)} %param.27) | copy-start | bytes 15364
  34.1 44.3 %collective-permute-start.5 = (bf16[3,64,128]{2,1,0:T(8,128)(2,1)S(1)}, bf16[3,64,128]{2,1,0:T(8,128)(2,1)S(1)}, u32[]{:S(2)}, u32[]{:S(2)}) collective-permute-start(bf16[3,64,128]{2,1,0:T(8,128)(2,1)S(1)} %bitcast.34), channel_id=1, source_target_pairs={{0,4},{4,0},{8,12},{12,8},{16,20},{20,16},{24,28},{28,24},{1,5},{5... | collective-permute-start | bytes 147464 | tf_op jit(solution)/shard_map/ppermute | solution.py:47
  38.3 40.1 %collective-permute-start.4 = (bf16[3,64,128]{2,1,0:T(8,128)(2,1)S(1)}, bf16[3,64,128]{2,1,0:T(8,128)(2,1)S(1)}, u32[]{:S(2)}, u32[]{:S(2)}) collective-permute-start(bf16[3,64,128]{2,1,0:T(8,128)(2,1)S(1)} %bitcast.33), channel_id=1, source_target_pairs={{4,8},{12,16},{20,24},{8,4},{16,12},{24,20},{5,9},{13,17},{21,25},... | collective-permute-start | bytes 147464 | tf_op jit(solution)/shard_map/ppermute | solution.py:46
  40.3 5.8 %collective-permute-start.8 = (bf16[640,128]{1,0:T(8,128)(2,1)S(1)}, bf16[640,128]{1,0:T(8,128)(2,1)S(1)}, u32[]{:S(2)}, u32[]{:S(2)}) collective-permute-start(bf16[640,128]{1,0:T(8,128)(2,1)S(1)} %pad_dynamic-slice_fusion), channel_id=1, source_target_pairs={{0,4},{4,0},{8,12},{12,8},{16,20},{20,16},{24,28},{28,24},{1,5},{5... | collective-permute-start | bytes 491528 | tf_op jit(solution)/shard_map/ppermute | solution.py:76
  46.2 5.0 %collective-permute-start.9 = (bf16[160,128]{1,0:T(8,128)(2,1)S(1)}, bf16[160,128]{1,0:T(8,128)(2,1)S(1)}, u32[]{:S(2)}, u32[]{:S(2)}) collective-permute-start(bf16[160,128]{1,0:T(8,128)(2,1)S(1)} %get-tuple-element.39), channel_id=1, source_target_pairs={{0,24},{4,28},{8,16},{12,20},{16,8},{20,12},{24,0},{28,4},{1,25},{... | collective-permute-start | bytes 122888 | tf_op jit(solution)/shard_map/ppermute | solution.py:76
  48.2 4.0 %collective-permute-start.11 = (bf16[160,128]{1,0:T(8,128)(2,1)S(1)}, bf16[160,128]{1,0:T(8,128)(2,1)S(1)}, u32[]{:S(2)}, u32[]{:S(2)}) collective-permute-start(bf16[160,128]{1,0:T(8,128)(2,1)S(1)} %get-tuple-element.40), channel_id=1, source_target_pairs={{0,8},{4,12},{8,0},{12,4},{16,24},{20,28},{24,16},{28,20},{1,9},{5... | collective-permute-start | bytes 122888 | tf_op jit(solution)/shard_map/ppermute | solution.py:76
  49.6 4.0 %collective-permute-start.10 = (bf16[160,128]{1,0:T(8,128)(2,1)S(1)}, bf16[160,128]{1,0:T(8,128)(2,1)S(1)}, u32[]{:S(2)}, u32[]{:S(2)}) collective-permute-start(bf16[160,128]{1,0:T(8,128)(2,1)S(1)} %get-tuple-element.41), channel_id=1, source_target_pairs={{0,16},{4,20},{8,24},{12,28},{16,0},{20,4},{24,8},{28,12},{1,17},{... | collective-permute-start | bytes 122888 | tf_op jit(solution)/shard_map/ppermute | solution.py:76
  53.6 24.9 %collective-permute-start.14 = (bf16[160,128]{1,0:T(8,128)(2,1)S(1)}, bf16[160,128]{1,0:T(8,128)(2,1)S(1)}, u32[]{:S(2)}, u32[]{:S(2)}) collective-permute-start(bf16[160,128]{1,0:T(8,128)(2,1)S(1)} %add_convert_fusion.2), channel_id=1, source_target_pairs={{0,3},{1,2},{2,1},{3,0},{4,7},{5,6},{6,5},{7,4},{8,11},{9,10},{10,... | collective-permute-start | bytes 122888 | tf_op jit(solution)/shard_map/ppermute | solution.py:79
  75.2 5.5 %collective-permute-start.13 = (bf16[160,128]{1,0:T(8,128)(2,1)S(1)}, bf16[160,128]{1,0:T(8,128)(2,1)S(1)}, u32[]{:S(2)}, u32[]{:S(2)}) collective-permute-start(bf16[160,128]{1,0:T(8,128)(2,1)S(1)} %add_convert_fusion.2), channel_id=1, source_target_pairs={{0,2},{1,3},{2,0},{3,1},{4,6},{5,7},{6,4},{7,5},{8,10},{9,11},{10,... | collective-permute-start | bytes 122888 | tf_op jit(solution)/shard_map/ppermute | solution.py:79
  77.9 4.0 %collective-permute-start.12 = (bf16[160,128]{1,0:T(8,128)(2,1)S(1)}, bf16[160,128]{1,0:T(8,128)(2,1)S(1)}, u32[]{:S(2)}, u32[]{:S(2)}) collective-permute-start(bf16[160,128]{1,0:T(8,128)(2,1)S(1)} %add_convert_fusion.2), channel_id=1, source_target_pairs={{0,1},{1,0},{2,3},{3,2},{4,5},{5,4},{6,7},{7,6},{8,9},{9,8},{10,11... | collective-permute-start | bytes 122888 | tf_op jit(solution)/shard_map/ppermute | solution.py:79
  82.0 7.9 %collective-permute-start.15 = (bf16[160,128]{1,0:T(8,128)(2,1)S(1)}, bf16[160,128]{1,0:T(8,128)(2,1)S(1)}, u32[]{:S(2)}, u32[]{:S(2)}) collective-permute-start(bf16[160,128]{1,0:T(8,128)(2,1)S(1)} %get-tuple-element.36), channel_id=1, source_target_pairs={{0,24},{4,28},{8,16},{12,20},{16,8},{20,12},{24,0},{28,4},{1,25},{... | collective-permute-start | bytes 122888 | tf_op jit(solution)/shard_map/ppermute | solution.py:91
  82.2 10.1 %collective-permute-start.6 = (bf16[64,128]{1,0:T(8,128)(2,1)S(1)}, bf16[64,128]{1,0:T(8,128)(2,1)S(1)}, u32[]{:S(2)}, u32[]{:S(2)}) collective-permute-start(bf16[64,128]{1,0:T(8,128)(2,1)S(1)} %get-tuple-element.50), channel_id=1, source_target_pairs={{1,2},{2,1},{5,6},{6,5},{9,10},{10,9},{13,14},{14,13},{17,18},{18,... | collective-permute-start | bytes 49160 | tf_op jit(solution)/shard_map/ppermute | solution.py:46
  82.8 9.4 %collective-permute-start.7 = (bf16[64,128]{1,0:T(8,128)(2,1)S(1)}, bf16[64,128]{1,0:T(8,128)(2,1)S(1)}, u32[]{:S(2)}, u32[]{:S(2)}) collective-permute-start(bf16[64,128]{1,0:T(8,128)(2,1)S(1)} %get-tuple-element.51), channel_id=1, source_target_pairs={{0,1},{1,0},{2,3},{3,2},{4,5},{5,4},{6,7},{7,6},{8,9},{9,8},{10,11... | collective-permute-start | bytes 49160 | tf_op jit(solution)/shard_map/ppermute | solution.py:47
  86.5 4.0 %collective-permute-start.16 = (bf16[160,128]{1,0:T(8,128)(2,1)S(1)}, bf16[160,128]{1,0:T(8,128)(2,1)S(1)}, u32[]{:S(2)}, u32[]{:S(2)}) collective-permute-start(bf16[160,128]{1,0:T(8,128)(2,1)S(1)} %get-tuple-element.36), channel_id=1, source_target_pairs={{0,16},{4,20},{8,24},{12,28},{16,0},{20,4},{24,8},{28,12},{1,17},{... | collective-permute-start | bytes 122888 | tf_op jit(solution)/shard_map/ppermute | solution.py:91
  88.2 4.0 %collective-permute-start.17 = (bf16[160,128]{1,0:T(8,128)(2,1)S(1)}, bf16[160,128]{1,0:T(8,128)(2,1)S(1)}, u32[]{:S(2)}, u32[]{:S(2)}) collective-permute-start(bf16[160,128]{1,0:T(8,128)(2,1)S(1)} %get-tuple-element.36), channel_id=1, source_target_pairs={{0,8},{4,12},{8,0},{12,4},{16,24},{20,28},{24,16},{28,20},{1,9},{5... | collective-permute-start | bytes 122888 | tf_op jit(solution)/shard_map/ppermute | solution.py:91
  92.2 1.5 %collective-permute-start.18 = (bf16[640,128]{1,0:T(8,128)(2,1)S(1)}, bf16[640,128]{1,0:T(8,128)(2,1)S(1)}, u32[]{:S(2)}, u32[]{:S(2)}) collective-permute-start(bf16[640,128]{1,0:T(8,128)(2,1)S(1)} %constant_dynamic-update-slice_fusion.2), channel_id=1, source_target_pairs={{0,4},{4,0},{8,12},{12,8},{16,20},{20,16},{24,28},{28,24},{1,5},{5... | collective-permute-start | bytes 491528 | tf_op jit(solution)/shard_map/ppermute | solution.py:91
  (7 other events, 298.2 us)
where the time goes:
time: 99.9 us; the launch traced here: 101 us
  starting transfers between devices  50.7 us (51%)
  Pallas kernels  20.9 us (21%)
  waiting for transfers between devices  9.93 us (10%)
  other arithmetic  9.03 us (9%)
  local copies, waits for them, and re-layouts  4.55 us (5%)
  between operations  4.18 us (4%)
  matrix products  2.04 us (2%)
    ppermute x3, starting transfers between devices, sum_everywhere(): lax.ppermute(total, 'gy', partners('gy', 1, mask)).astype(jnp.float32)  24.8 us
    pallas_call x1, Pallas kernels, layer_call(): pl.pallas_call(functools.partial(layer_kernel, halo), out_shape=(jax.Shap...  20.9 us
    ppermute x4, starting transfers between devices, sum_everywhere(): lax.ppermute(piece, 'gx', partners('gx', stride, mask)).astype(jnp.float32)  8.36 us
    ppermute x2, starting transfers between devices, returned_along(): from_near = lax.ppermute(jnp.where(even, high, low), axis, near)  7.84 us
    ppermute x4, waiting for transfers between devices, sum_everywhere(): lax.ppermute(piece, 'gx', partners('gx', stride, mask)).astype(jnp.float32)  3.81 us
    ppermute x4, starting transfers between devices, sum_everywhere(): piece = lax.ppermute(total, 'gx', partners('gx', stride, mask))  3.62 us
    ppermute x2, starting transfers between devices, extended(): from_near = lax.ppermute(block, axis, near)  3.5 us
    ppermute x3, waiting for transfers between devices, sum_everywhere(): lax.ppermute(total, 'gy', partners('gy', 1, mask)).astype(jnp.float32)  3.47 us
  transfers between devices with their start and end apart: 19, of which 10 were waited for; matrix products, arithmetic and copies ran while one was open for 7% of the time, Pallas kernels for 0%

commit v1 on v0

v1 whole, which is shorter than its diff:
```python
import functools

import jax
import jax.numpy as jnp
from jax import lax
from jax.experimental import pallas as pl
from jax.experimental.pallas import tpu as pltpu
from jax.sharding import PartitionSpec as P

STEP = 10


first_decay = 0.5
second_decay = 0.5
adam_epsilon = 1e-08
weight_decay = 0.01
matrix_rate = 0.05
vector_rate = 0.2
average_decay = 0.9
clip_norm = 1.0
norm_epsilon = 1e-05


def neighbour_pairs(count):
    near = [(i, i ^ 1) for i in range(count) if (i ^ 1) < count]
    far = [(i, i + 1) for i in range(1, count - 1, 2)]
    return near, far + [(target, source) for source, target in far]


def stages(count):
    result, stride = [], 1
    while stride < count:
        factor = 2 if stride == 1 else min(4, count // stride)
        result.append((stride, factor))
        stride *= factor
    return result


def selector(indices, width, dtype):
    columns = lax.broadcasted_iota(jnp.int32, (indices.shape[0], width), 1)
    return (indices[:, None] == columns).astype(dtype)


def adamw(param, grad, moment, second, average, scale, rate):
    clipped = grad * scale
    moment_new = first_decay * moment + (1.0 - first_decay) * clipped
    second_new = second_decay * second + (1.0 - second_decay) * clipped * clipped
    corrected = moment_new / (1.0 - first_decay**STEP)
    denom = jnp.sqrt(second_new / (1.0 - second_decay**STEP)) + adam_epsilon
    param_new = param - rate * (corrected / denom + weight_decay * param)
    average_new = average_decay * average + (1.0 - average_decay) * param_new
    return (moment_new, second_new, param_new, average_new)


CHUNK = 16
GROUP = 32
TILE = CHUNK * GROUP
LANES = 128
PIECES = 8


def dot(left, right):
    return jnp.dot(left, right, preferred_element_type=jnp.float32)


def dot_nt(left, right):
    return lax.dot_general(
        left, right, (((1,), (1,)), ((), ())), preferred_element_type=jnp.float32
    )


def dot_tn(left, right):
    return lax.dot_general(
        left, right, (((0,), (0,)), ((), ())), preferred_element_type=jnp.float32
    )


def split_pair(values, axis=1):
    high = values.astype(jnp.bfloat16)
    low = (values - high.astype(jnp.float32)).astype(jnp.bfloat16)
    return jnp.concatenate([high, low], axis=axis)


def halves(pair):
    width = pair.shape[1] // 2
    return pair[:, :width] + pair[:, width:]


def silu_of_half(half):
    turn = jnp.tanh(half)
    lift = 1.0 + turn
    act = half * lift
    return act, lift + act * (1.0 - turn)


def row_sum(values):
    return jnp.sum(values, axis=-1, keepdims=True)


def scaled_unit(values, width):
    center = values - row_sum(values) * (1.0 / width)
    inverse = lax.rsqrt(row_sum(center * center) + width * norm_epsilon)
    return center * inverse, inverse


def scaled_unit_back(scaled, unit, inverse, width):
    shift = row_sum(scaled) * (1.0 / width)
    return inverse * (scaled - shift - unit * row_sum(scaled * unit))


def column_total(values):
    return jnp.sum(values, axis=0, keepdims=True)


def iota(shape, dim):
    return lax.broadcasted_iota(jnp.int32, shape, dim)


def layer_kernel(
    halo,
    count_ref,
    neighbour_ref,
    mask_ref,
    latents_ref,
    ring_ref,
    ring_far_ref,
    ring_near_ref,
    upstream_ref,
    vectors_ref,
    weights_hbm,
    edges_hbm,
    cotangent_hbm,
    nodes_out_ref,
    edges_out_hbm,
    edges_grad_hbm,
    node_part_ref,
    halo_far_ref,
    halo_near_ref,
    halo_own_ref,
    grads_send_ref,
    grads_keep_ref,
    edges_buf,
    cotangent_buf,
    kept_edges,
    kept_index,
    kept_act1,
    kept_act2,
    kept_slope1,
    kept_slope2,
    kept_unit,
    kept_inverse,
    weights_buf,
    low_ref,
    table_ref,
    gather_ref,
    receiver_ref,
    receiver_tile,
    neighbour_rows,
    segment_ref,
    blocks_ref,
    chunk_sums,
    chunk_grads,
    index_acc,
    mat_acc,
    vec_acc,
    first_tile,
    third_tile,
    passed_tile,
    halo_grad,
    grads,
    list_rows,
    listed,
    in_sems,
    out_sems,
    list_sem,
    weights_sem,
):
    f32, bf16, i32 = jnp.float32, jnp.bfloat16, jnp.int32
    slots, particles = neighbour_ref.shape
    per = slots // CHUNK
    chunks = particles * per
    width = latents_ref.shape[1]
    rows = table_ref.shape[0]
    piece = chunks // PIECES
    root = float(width) ** 0.5
    odd_x = lax.axis_index("gx") & 1
    odd_y = lax.axis_index("gy") & 1

    fetch_weights = pltpu.make_async_copy(weights_hbm, weights_buf, weights_sem)
    fetch_weights.start()
    loads = [
        [
            pltpu.make_async_copy(
                source.at[pl.ds(p * piece, piece)],
                target.at[pl.ds(p * piece, piece)],
                in_sems.at[order * PIECES + p],
            )
            for p in range(PIECES)
        ]
        for order, (source, target) in enumerate(
            ((edges_hbm, edges_buf), (cotangent_hbm, cotangent_buf))
        )
    ]
    for copy in loads[0] + loads[1]:
        copy.start()
    edges_buf[chunks] = jnp.zeros((CHUNK, width), bf16)
    cotangent_buf[chunks] = jnp.zeros((CHUNK, width), bf16)

    mask = mask_ref[...].astype(f32)
    degree = jnp.sum(mask, axis=0, keepdims=True)
    taken = ((degree.astype(i32) + (CHUNK - 1)) >> 4).astype(f32)
    earlier = iota((particles, particles), 0) < iota((particles, particles), 1)
    begin = dot(jnp.broadcast_to(taken, (16, particles)).astype(bf16), earlier.astype(bf16))
    degree_col = dot_tn(mask.astype(bf16), jnp.ones((slots, width), bf16))
    taken_col = ((degree_col.astype(i32) + (CHUNK - 1)) >> 4).astype(f32)
    later = iota((particles, particles), 1) < iota((particles, particles), 0)
    begin_col = dot(later.astype(bf16), taken_col.astype(bf16))
    end_col = begin_col + taken_col
    for block in range(chunks // width):
        lane = iota((particles, width), 1).astype(f32) + block * width
        segment_ref[:, block * width : (block + 1) * width] = (
            (lane >= begin_col) & (lane < end_col)
        ).astype(bf16)
    total = row_sum(taken)
    who = iota((16, particles), 1).astype(f32)
    offset = per * who - begin
    coarse = jnp.floor(offset * 0.125) * 8.0
    line = iota((16, particles), 0)
    facts = jnp.where(
        line == 0,
        who,
        jnp.where(line == 1, coarse, jnp.where(line == 2, offset - coarse, degree)),
    )
    listing = dot(facts.astype(bf16), segment_ref[...])
    place = iota((1, chunks), 1).astype(f32)
    particle = listing[0:1, :]
    chunk = listing[1:2, :] + listing[2:3, :] + place
    rest = listing[3:4, :] - CHUNK * (chunk - per * particle)
    used = place < total
    list_rows[...] = jnp.zeros(list_rows.shape, i32)
    list_rows[0:1, 0:chunks] = jnp.where(used, chunk, float(chunks)).astype(i32)
    list_rows[0:1, chunks:] = jnp.full((1, list_rows.shape[1] - chunks), chunks, i32)
    list_rows[1:2, 0:chunks] = jnp.where(used, particle, float(particles)).astype(i32)
    list_rows[1:2, chunks:] = jnp.full((1, list_rows.shape[1] - chunks), particles, i32)
    list_rows[2:3, 0:chunks] = jnp.where(used, rest, 0.0).astype(i32)
    list_rows[3:4, 0:particles] = jnp.broadcast_to(total, (1, particles)).astype(i32)
    list_rows[4:5, 0:particles] = (begin[0:1, :] + taken).astype(i32)
    fetch_list = pltpu.make_async_copy(list_rows, listed, list_sem)
    fetch_list.start()

    neighbour = neighbour_ref[...]
    neighbour = jnp.where(neighbour >= particles + 5 * halo, neighbour - halo, neighbour)
    neighbour_rows[...] = jnp.zeros(neighbour_rows.shape, f32)
    neighbour_rows[0:particles, 0:slots] = neighbour.astype(f32).T

    block_of = iota((TILE, LANES), 0) >> 4
    for quarter in range(LANES // GROUP):
        blocks_ref[quarter] = (iota((TILE, LANES), 1) == block_of + quarter * GROUP).astype(bf16)
    chunk_sums[...] = jnp.zeros(chunk_sums.shape, f32)
    chunk_grads[...] = jnp.zeros(chunk_grads.shape, f32)
    index_acc[...] = jnp.zeros(index_acc.shape, f32)
    mat_acc[...] = jnp.zeros(mat_acc.shape, f32)
    vec_acc[...] = jnp.zeros(vec_acc.shape, f32)
    gather_ref[rows + width :, :] = jnp.zeros((LANES, 2 * width), bf16)
    tail = low_ref.shape[0] * width
    grads[tail:, :] = jnp.zeros((grads.shape[0] - tail, width), f32)

    table_ref[0:particles, :] = latents_ref[...]
    far, near, own = ring_far_ref[...], ring_near_ref[...], ring_ref[...]
    low_y = jnp.where(odd_y == 0, far, near)
    high_y = jnp.where(odd_y == 0, near, far)
    spot = particles
    for a in range(3):
        for b, strip in enumerate((low_y, own, high_y)):
            if a == 1 and b == 1:
                continue
            if a == 1:
                part = strip[2 * halo :]
            elif a == 0:
                part = jnp.where(odd_x == 0, strip[0:halo], strip[halo : 2 * halo])
            else:
                part = jnp.where(odd_x == 0, strip[halo : 2 * halo], strip[0:halo])
            table_ref[spot : spot + halo, :] = part
            spot += halo

    vectors = vectors_ref[...]

    def vector(row):
        return vectors[row : row + 1, :]

    fetch_weights.wait()
    for block in range(low_ref.shape[0]):
        low_ref[block] = weights_buf[block].astype(bf16)
    half3 = (0.5 * low_ref[3].astype(f32)).astype(bf16)
    half4 = (0.5 * low_ref[4].astype(f32)).astype(bf16)
    latents = latents_ref[...]
    gather_ref[0:rows, :] = split_pair(0.5 * dot(table_ref[...], low_ref[2]))
    gather_ref[rows : rows + width, :] = jnp.concatenate(
        [(0.5 * low_ref[0].astype(f32)).astype(bf16), jnp.zeros((width, width), bf16)], axis=1
    )
    receiver_ref[0:particles, :] = 0.5 * (dot(latents, low_ref[1]) + vector(0))
    receiver_ref[particles:, :] = jnp.zeros((receiver_ref.shape[0] - particles, width), f32)

    fetch_list.wait()
    tiles = (listed[3, 0] + (GROUP - 1)) >> 5
    for copy in loads[0]:
        copy.wait()

    sublane = iota((CHUNK, width), 0)
    diagonal = iota((CHUNK, width), 1) - sublane
    lane16 = iota((TILE, width), 1).astype(jnp.int16)

    def flat(ref, t):
        return ref[pl.ds(t * GROUP, GROUP)].reshape(TILE, width)

    def keep(ref, t, values):
        ref[pl.ds(t * GROUP, GROUP)] = values.astype(ref.dtype).reshape(GROUP, CHUNK, width)

    def span(j):
        return slice(j * CHUNK, (j + 1) * CHUNK)

    def one_hot(t):
        index = flat(kept_index, t)
        return [
            jnp.where(index == lane16 + jnp.int16(b * width), bf16(1), bf16(0))
            for b in range(rows // width)
        ]

    def gather(t):
        base = t * GROUP
        for j in range(GROUP):
            chunk, particle = listed[0, base + j], listed[1, base + j]
            kept_edges[base + j] = edges_buf[chunk]
            row = jnp.broadcast_to(neighbour_rows[pl.ds(particle, 1), :], (CHUNK, width))
            start = (chunk & (per - 1)) * CHUNK
            index = row_sum(jnp.where(diagonal == start, row, 0.0))
            kept_index[base + j] = (
                jnp.broadcast_to(index, (CHUNK, width)).astype(i32).astype(jnp.int16)
            )
            receiver_tile[j : j + 1, :] = receiver_ref[pl.ds(particle, 1), :]
        gather_ref[rows + width : rows + width + GROUP, :] = split_pair(receiver_tile[...])
        picks = jnp.concatenate(one_hot(t) + [flat(kept_edges, t), blocks_ref[0]], axis=1)
        first_tile[...] = halves(dot(picks, gather_ref[...]))

    gain_root = vector(3) * root

    def forward(t, carry):
        base = t * GROUP
        act, slope = silu_of_half(first_tile[...])
        act = act.astype(bf16)
        keep(kept_act1, t, act)
        keep(kept_slope1, t, slope)
        gather(t + 1)
        act, slope = silu_of_half(dot(act, half3) + 0.5 * vector(1))
        act = act.astype(bf16)
        keep(kept_act2, t, act)
        keep(kept_slope2, t, slope)
        unit, inverse = scaled_unit(dot(act, low_ref[4]) + vector(2), width)
        keep(kept_unit, t, unit)
        keep(kept_inverse, t, jnp.broadcast_to(inverse, (TILE, width)))
        change = unit * gain_root + vector(4)
        for j in range(GROUP):
            chunk = listed[0, base + j]
            alive = sublane < listed[2, base + j]
            fresh = kept_edges[base + j].astype(f32) + jnp.where(alive, change[span(j)], 0.0)
            edges_buf[chunk] = fresh.astype(bf16)
            chunk_sums[pl.ds(base + j, 1), :] = column_total(jnp.where(alive, fresh, 0.0))
        return carry

    gather(0)
    lax.fori_loop(0, tiles, forward, 0)
    keep(kept_unit, tiles, jnp.zeros((TILE, width), f32))

    stores = [
        pltpu.make_async_copy(
            edges_buf.at[pl.ds(p * piece, piece)],
            edges_out_hbm.at[pl.ds(p * piece, piece)],
            out_sems.at[p],
        )
        for p in range(PIECES)
    ]
    for copy in stores:
        copy.start()

    aggregate = halves(dot(segment_ref[...], split_pair(chunk_sums[...]))).astype(bf16)
    half1 = 0.5 * (dot(latents, low_ref[5]) + dot(aggregate, low_ref[6]) + vector(5))
    act1, slope1 = silu_of_half(half1)
    act1 = act1.astype(bf16)
    act2, slope2 = silu_of_half(0.5 * (dot(act1, low_ref[7]) + vector(6)))
    act2 = act2.astype(bf16)
    unit, inverse = scaled_unit(dot(act2, low_ref[8]) + vector(7), width)
    alive = (iota((particles, width), 0) < count_ref[0]).astype(f32)
    upstream = upstream_ref[...].astype(f32)
    nodes_out_ref[...] = (
        latents.astype(f32) + alive * (unit * (vector(8) * root) + vector(9))
    ).astype(bf16)
    held = alive * upstream
    third = scaled_unit_back(held * (vector(8) * root), unit, inverse, width).astype(bf16)
    second = (0.5 * slope2 * dot_nt(third, low_ref[8])).astype(bf16)
    first = (0.5 * slope1 * dot_nt(second, low_ref[7])).astype(bf16)
    receiver_ref[0:particles, :] = dot_nt(first, low_ref[6])
    node_part_ref[...] = upstream + dot_nt(first, low_ref[5])

    def put_block(block, values):
        grads[block * width : (block + 1) * width, :] = values

    put_block(5, dot_tn(latents, first))
    put_block(6, dot_tn(aggregate, first))
    put_block(7, dot_tn(act1, second))
    put_block(8, dot_tn(act2, third))
    for row, values in enumerate(
        (first.astype(f32), second.astype(f32), third.astype(f32), held * unit * root, held)
    ):
        grads[tail + 5 + row : tail + 6 + row, :] = column_total(values)

    for copy in loads[1]:
        copy.wait()

    def add_columns(row, values):
        vec_acc[8 * row : 8 * row + 8, :] += jnp.sum(values.reshape(TILE // 8, 8, width), axis=0)

    def descend(t):
        base = t * GROUP
        parts = []
        for j in range(GROUP):
            chunk, particle = listed[0, base + j], listed[1, base + j]
            alive = sublane < listed[2, base + j]
            passed = cotangent_buf[chunk].astype(f32) + jnp.where(
                alive, receiver_ref[pl.ds(particle, 1), :], 0.0
            )
            passed_tile[t & 1, span(j), :] = passed
            parts.append(jnp.where(alive, passed, 0.0))
        held = jnp.concatenate(parts, axis=0)
        unit = flat(kept_unit, t).astype(f32)
        third = scaled_unit_back(held * gain_root, unit, flat(kept_inverse, t), width)
        third_tile[...] = third.astype(bf16)
        return held, unit, third

    def backward(t, carry):
        base = t * GROUP
        third = third_tile[...]
        third_f32 = third.astype(f32)
        second = 1.0 * flat(kept_slope2, t).astype(f32) * dot_nt(third, half4)
        add_columns(1, second)
        add_columns(2, third_f32)
        second = second.astype(bf16)
        mat_acc[1] += dot_tn(flat(kept_act2, t), third)
        held, unit, _ = descend(t + 1)
        add_columns(3, held * unit)
        add_columns(4, held)
        first = (flat(kept_slope1, t).astype(f32) * dot_nt(second, half3)).astype(bf16)
        result = passed_tile[t & 1] + dot_nt(first, low_ref[0])
        for j in range(GROUP):
            cotangent_buf[listed[0, base + j]] = result[span(j)].astype(bf16)
        mat_acc[0] += dot_tn(flat(kept_act1, t), second)
        picks = jnp.concatenate(one_hot(t) + [flat(kept_edges, t), blocks_ref[t & 3]], axis=1)
        index_acc[...] += dot_tn(first, picks[:, 0 : rows + width])
        chunk_grads[t >> 2] += dot_tn(first, picks[:, rows + width :])
        return carry

    held, unit, _ = descend(0)
    add_columns(3, held * unit)
    add_columns(4, held)
    results = [
        pltpu.make_async_copy(
            cotangent_buf.at[pl.ds(p * piece, piece)],
            edges_grad_hbm.at[pl.ds(p * piece, piece)],
            out_sems.at[PIECES + p],
        )
        for p in range(PIECES)
    ]
    lax.fori_loop(0, tiles, backward, 0)
    for copy in results:
        copy.start()

    stacked = split_pair(
        jnp.concatenate([chunk_grads[g] for g in range(chunk_grads.shape[0])], axis=1), axis=0
    )
    receiver_grad = halves(dot_nt(segment_ref[...], stacked)).astype(bf16)
    grads[tail : tail + 1, :] = halves(dot_nt(jnp.ones((8, chunks), bf16), stacked))[0:1, :]
    for row in range(1, 5):
        values = column_total(vec_acc[8 * row : 8 * row + 8, :])
        grads[tail + row : tail + row + 1, :] = values * root if row == 3 else values
    sent = index_acc[:, 0:rows].astype(bf16)
    put_block(0, index_acc[:, rows:].T)
    put_block(1, dot_tn(latents, receiver_grad))
    put_block(2, dot(sent, table_ref[...]).T)
    put_block(3, mat_acc[0])
    put_block(4, mat_acc[1])
    table_grad = lax.dot_general(
        sent, low_ref[2], (((0,), (1,)), ((), ())), preferred_element_type=f32
    )
    node_part_ref[...] += dot_nt(receiver_grad, low_ref[1]) + table_grad[0:particles, :]
    halo_grad[...] = table_grad[particles:, :].astype(bf16)
    low_x = halo_grad[0 : 3 * halo, :]
    high_x = halo_grad[5 * halo : 8 * halo, :]
    halo_far_ref[...] = jnp.where(odd_x == 0, low_x, high_x)
    halo_near_ref[...] = jnp.where(odd_x == 0, high_x, low_x)
    halo_own_ref[...] = halo_grad[3 * halo : 5 * halo, :]
    part_rows = grads_keep_ref.shape[0]
    lower, upper = grads[0:part_rows, :], grads[part_rows:, :]
    grads_keep_ref[...] = jnp.where(odd_x == 0, lower, upper)
    grads_send_ref[...] = jnp.where(odd_x == 0, upper, lower).astype(bf16)

    for copy in stores + results:
        copy.wait()


def layer_call(
    halo, grad_rows, counts, neighbours, edge_mask, latents, ring, ring_far, ring_near, upstream,
    vectors, weights, edges, cotangents,
):
    f32, bf16, i32 = jnp.float32, jnp.bfloat16, jnp.int32
    particles, slots = neighbours.shape
    width = latents.shape[1]
    rows = particles + 8 * halo
    chunks = particles * slots // CHUNK
    whole = pl.BlockSpec(memory_space=pltpu.VMEM)
    outside = pl.BlockSpec(memory_space=pl.ANY)
    edge_shape = (chunks, CHUNK, width)
    kept_shape = (chunks + GROUP, CHUNK, width)
    kept = pltpu.VMEM(kept_shape, bf16)
    buffer = pltpu.VMEM((chunks + 1, CHUNK, width), bf16)
    strip = jax.ShapeDtypeStruct((3 * halo, width), bf16)
    return pl.pallas_call(
        functools.partial(layer_kernel, halo),
        out_shape=(
            jax.ShapeDtypeStruct((particles, width), bf16),
            jax.ShapeDtypeStruct(edge_shape, bf16),
            jax.ShapeDtypeStruct(edge_shape, bf16),
            jax.ShapeDtypeStruct((particles, width), f32),
            strip,
            strip,
            jax.ShapeDtypeStruct((2 * halo, width), bf16),
            jax.ShapeDtypeStruct((grad_rows // 2, width), bf16),
            jax.ShapeDtypeStruct((grad_rows // 2, width), f32),
        ),
        in_specs=[pl.BlockSpec(memory_space=pltpu.SMEM)] + [whole] * 8 + [outside] * 3,
        out_specs=(whole, outside, outside, whole, whole, whole, whole, whole, whole),
        scratch_shapes=[
            buffer,
            buffer,
            kept,
            pltpu.VMEM(kept_shape, jnp.int16),
            kept,
            kept,
            kept,
            kept,
            kept,
            pltpu.VMEM(kept_shape, f32),
            pltpu.VMEM(weights.shape, f32),
            pltpu.VMEM(weights.shape, bf16),
            pltpu.VMEM((rows, width), bf16),
            pltpu.VMEM((rows + width + LANES, 2 * width), bf16),
            pltpu.VMEM((particles + 8, width), f32),
            pltpu.VMEM((GROUP, width), f32),
            pltpu.VMEM((particles + 8, width), f32),
            pltpu.VMEM((particles, chunks), bf16),
            pltpu.VMEM((LANES // GROUP, TILE, LANES), bf16),
            pltpu.VMEM((chunks, width), f32),
            pltpu.VMEM((chunks // LANES, width, LANES), f32),
            pltpu.VMEM((width, rows + width), f32),
            pltpu.VMEM((2, width, width), f32),
            pltpu.VMEM((40, width), f32),
            pltpu.VMEM((TILE, width), f32),
            pltpu.VMEM((TILE, width), bf16),
            pltpu.VMEM((2, TILE, width), f32),
            pltpu.VMEM((8 * halo, width), bf16),
            pltpu.VMEM((grad_rows, width), f32),
            pltpu.VMEM((8, chunks + LANES), i32),
            pltpu.SMEM((8, chunks + LANES), i32),
            pltpu.SemaphoreType.DMA((2 * PIECES,)),
            pltpu.SemaphoreType.DMA((2 * PIECES,)),
            pltpu.SemaphoreType.DMA,
            pltpu.SemaphoreType.DMA,
        ],
        compiler_params=pltpu.CompilerParams(vmem_limit_bytes=60 * 1024 * 1024),
        name="edge_layer",
    )(
        counts,
        neighbours.T,
        edge_mask.T,
        latents,
        ring,
        ring_far,
        ring_near,
        upstream,
        vectors,
        weights,
        edges.reshape(edge_shape),
        cotangents.reshape(edge_shape),
    )


def update_kernel(
    mine_ref,
    other_ref,
    weights_ref,
    vectors_ref,
    weights_m_ref,
    vectors_m_ref,
    weights_v_ref,
    vectors_v_ref,
    weights_ema_ref,
    vectors_ema_ref,
    norm_ref,
    weights_m_out,
    vectors_m_out,
    weights_v_out,
    vectors_v_out,
    weights_out,
    vectors_out,
    weights_copy_out,
    vectors_copy_out,
    weights_ema_out,
    vectors_ema_out,
    grads,
):
    f32 = jnp.float32
    odd = lax.axis_index("gx") & 1
    part_rows, width = mine_ref.shape
    mine, other = mine_ref[...].astype(f32), other_ref[...].astype(f32)
    grads[0:part_rows, :] = jnp.where(odd == 0, mine, other)
    grads[part_rows:, :] = jnp.where(odd == 0, other, mine)
    squares = jnp.sum((mine * mine + other * other).reshape(part_rows // 8, 8, width), axis=0)
    norm = jnp.sqrt(jnp.sum(jnp.sum(squares, axis=1, keepdims=True), axis=0, keepdims=True))
    norm_ref[...] = norm
    scale = clip_norm / jnp.maximum(norm, clip_norm)
    for block in range(weights_ref.shape[0]):
        moment, second, param, average = adamw(
            weights_ref[block],
            grads[block * width : (block + 1) * width, :],
            weights_m_ref[block],
            weights_v_ref[block],
            weights_ema_ref[block],
            scale,
            matrix_rate,
        )
        weights_m_out[block] = moment
        weights_v_out[block] = second
        weights_out[block] = param
        weights_copy_out[block] = param.astype(jnp.bfloat16)
        weights_ema_out[block] = average
    tail = weights_ref.shape[0] * width
    moment, second, param, average = adamw(
        vectors_ref[...],
        grads[tail : tail + vectors_ref.shape[0], :],
        vectors_m_ref[...],
        vectors_v_ref[...],
        vectors_ema_ref[...],
        scale,
        vector_rate,
    )
    vectors_m_out[...] = moment
    vectors_v_out[...] = second
    vectors_out[...] = param
    vectors_copy_out[...] = param.astype(jnp.bfloat16)
    vectors_ema_out[...] = average


def update_call(mine, other, weights, vectors, weights_m, vectors_m, weights_v, vectors_v,
                weights_ema, vectors_ema):
    f32, bf16 = jnp.float32, jnp.bfloat16
    mat, vec = weights.shape, vectors.shape
    kinds = (
        ((1, 1), f32), (mat, f32), (vec, f32), (mat, f32), (vec, f32), (mat, f32), (vec, f32),
        (mat, bf16), (vec, bf16), (mat, f32), (vec, f32),
    )
    whole = pl.BlockSpec(memory_space=pltpu.VMEM)
    return pl.pallas_call(
        update_kernel,
        out_shape=tuple(jax.ShapeDtypeStruct(*kind) for kind in kinds),
        in_specs=[whole] * 10,
        out_specs=(whole,) * 11,
        scratch_shapes=[pltpu.VMEM((2 * mine.shape[0], mine.shape[1]), f32)],
        compiler_params=pltpu.CompilerParams(vmem_limit_bytes=24 * 1024 * 1024),
        name="update",
    )(mine, other, weights, vectors, weights_m, vectors_m, weights_v, vectors_v, weights_ema,
      vectors_ema)


def pair_exchange(to_far, to_near, axis):
    near, far = neighbour_pairs(lax.axis_size(axis))
    return lax.ppermute(to_far, axis, far), lax.ppermute(to_near, axis, near)


def partners(axis, stride, mask):
    return [(i, i ^ (mask * stride)) for i in range(lax.axis_size(axis))]


def per_device(
    node_latents,
    edge_latents,
    node_cotangent,
    edge_cotangent,
    neighbours,
    edge_mask,
    send_table,
    counts,
    weights,
    vectors,
    weights_m,
    vectors_m,
    weights_v,
    vectors_v,
    weights_ema,
    vectors_ema,
):
    f32, bf16 = jnp.float32, jnp.bfloat16
    tok_rows, width = node_latents.shape
    halo = send_table.shape[1]
    boundary_pick = selector(send_table[0], tok_rows, bf16)
    boundary = jnp.dot(boundary_pick, node_latents, preferred_element_type=f32).astype(bf16)
    from_far, from_near = pair_exchange(boundary, boundary, "gx")
    ring = jnp.concatenate([from_far, from_near, boundary], axis=0)
    ring_far, ring_near = pair_exchange(ring, ring, "gy")
    unit = 16 * lax.axis_size("gx")
    grad_rows = -(-(weights.shape[0] * width + vectors.shape[0]) // unit) * unit
    (
        nodes_out,
        edges_out,
        edges_in_grad,
        node_part,
        halo_far,
        halo_near,
        halo_own,
        grads_send,
        grads_keep,
    ) = layer_call(
        halo, grad_rows, counts, neighbours, edge_mask, node_latents, ring, ring_far, ring_near,
        node_cotangent, vectors, weights, edge_latents, edge_cotangent,
    )
    index = lax.axis_index("gx")
    got = lax.ppermute(grads_send, "gx", partners("gx", 1, 1))
    total = (grads_keep + got.astype(f32)).astype(bf16)
    split = stages(lax.axis_size("gx"))[1:]
    for stride, factor in split:
        part = (index // stride) % factor
        height = total.shape[0] // factor
        mine = lax.dynamic_slice_in_dim(total, part * height, height, 0).astype(f32)
        for mask in range(factor - 1, 0, -1):
            piece = lax.dynamic_slice_in_dim(total, (part ^ mask) * height, height, 0)
            mine = mine + lax.ppermute(piece, "gx", partners("gx", stride, mask)).astype(f32)
        total = mine.astype(bf16)
    total, halo_far, halo_near = lax.optimization_barrier((total, halo_far, halo_near))
    back_far, back_near = pair_exchange(halo_far, halo_near, "gx")
    terms = [total.astype(f32)] + [
        lax.ppermute(total, "gy", partners("gy", 1, mask)).astype(f32)
        for mask in range(1, lax.axis_size("gy"))
    ]
    while len(terms) > 1:
        terms = [terms[i] + terms[i + 1] for i in range(0, len(terms), 2)]
    total = terms[0].astype(bf16)
    strips = back_far.astype(f32) + back_near.astype(f32)
    strips = strips + jnp.concatenate(
        [halo_own[:halo], jnp.zeros((halo, width), bf16), halo_own[halo:]], axis=0
    ).astype(f32)
    even_y = lax.axis_index("gy") % 2 == 0
    low_y, high_y = strips[:halo].astype(bf16), strips[2 * halo :].astype(bf16)
    total, low_y, high_y = lax.optimization_barrier((total, low_y, high_y))
    last_far, last_near = pair_exchange(
        jnp.where(even_y, low_y, high_y), jnp.where(even_y, high_y, low_y), "gy"
    )
    for stride, factor in reversed(split):
        part = (index // stride) % factor
        height = total.shape[0]
        joined = jnp.zeros((factor * height, width), bf16)
        joined = lax.dynamic_update_slice_in_dim(joined, total, part * height, 0)
        for mask in range(factor - 1, 0, -1):
            piece = lax.ppermute(total, "gx", partners("gx", stride, mask))
            joined = lax.dynamic_update_slice_in_dim(joined, piece, (part ^ mask) * height, 0)
        total = joined
    other = lax.ppermute(total, "gx", partners("gx", 1, 1))
    boundary_grad = strips[halo : 2 * halo] + last_far.astype(f32) + last_near.astype(f32)
    returned = lax.dot_general(
        boundary_pick.astype(f32),
        boundary_grad,
        (((0,), (0,)), ((), ())),
        precision=lax.Precision.HIGHEST,
        preferred_element_type=f32,
    )
    nodes_in_grad = (node_part + returned).astype(bf16)
    updated = update_call(
        total, other, weights, vectors, weights_m, vectors_m, weights_v, vectors_v, weights_ema,
        vectors_ema,
    )
    return (
        nodes_out,
        edges_out.reshape(edge_latents.shape),
        nodes_in_grad,
        edges_in_grad.reshape(edge_latents.shape),
        updated[0].reshape(()),
    ) + tuple(updated[1:])


def solution(mesh):
    in_specs = (
        P(("gx", "gy"), None),
        P(("gx", "gy"), None, None),
        P(("gx", "gy"), None),
        P(("gx", "gy"), None, None),
        P(("gx", "gy"), None),
        P(("gx", "gy"), None),
        P(("gx", "gy"), None),
        P(("gx", "gy")),
        P(),
        P(),
        P(),
        P(),
        P(),
        P(),
        P(),
        P(),
    )
    out_specs = (
        P(("gx", "gy"), None),
        P(("gx", "gy"), None, None),
        P(("gx", "gy"), None),
        P(("gx", "gy"), None, None),
        P(),
        P(),
        P(),
        P(),
        P(),
        P(),
        P(),
        P(),
        P(),
        P(),
        P(),
    )
    return jax.shard_map(
        per_device, mesh=mesh, in_specs=in_specs, out_specs=out_specs, check_vma=False
    )
```

time: 99.9 us -> 86.8 us (0.87); the launches traced: 101 us -> 86.7 us
  other arithmetic: 9.03 us -> 2.72 us
  local copies, waits for them, and re-layouts: 4.55 us -> 1.6 us
  between operations: 4.18 us -> 1.58 us
  waiting for transfers between devices: 9.93 us -> 7.44 us
  starting transfers between devices: 50.7 us -> 52.1 us
  Pallas kernels: 20.9 us -> 19.8 us
    pallas_call x1, Pallas kernels: 20.9 us -> 17.7 us  [layer_call(): pl.pallas_call(functools.partial(layer_kernel, halo), out_shape=(jax.Shap...]
    unnamed x26 -> x24, local copies, waits for them, and re-layouts: 3.34 us -> 0.68 us
    ppermute x19, waiting for transfers between devices: 9.93 us -> 7.44 us  [the longest x8 3.65 us: pair_exchange(): return (lax.ppermute(to_far, axis, far), lax.ppermute(to_near, axis, near))]
    add x2 -> x0, other arithmetic: 2.22 us -> none  [adamw(): average_new = average_decay * average + (1.0 - average_decay) * param_new]
    pallas_call x0 -> x1, Pallas kernels: none -> 2.05 us  [update_call(): pl.pallas_call(update_kernel, out_shape=tuple((jax.ShapeDtypeStruct(*kind...]
    concatenate x4 -> x1, other arithmetic: 1.65 us -> 0.01 us  [per_device(): ring = jnp.concatenate([from_far, from_near, boundary], axis=0)]
    ppermute x19, starting transfers between devices: 50.7 us -> 52.1 us  [the longest x3 17.8 us: per_device(): lax.ppermute(total, 'gy', partners('gy', 1, mask)).astype(f32)]
    reduce_sum x2 -> x0, other arithmetic: 1.35 us -> none  [the longest x1 0.75 us: per_device(): jnp.sum(grad_mats * grad_mats) + jnp.sum(grad_vecs * grad_vecs)]
  transfers between devices with their start and end apart: 19 -> 19, of which waited for: 10 -> 7; matrix products, arithmetic and copies ran while one was open for 7% -> 3% of each run, Pallas kernels for 0% -> 0%
where the time goes in v1:
time: 86.8 us; the launch traced here: 86.7 us
  starting transfers between devices  52.1 us (60%)
  Pallas kernels  19.8 us (23%)
  waiting for transfers between devices  7.44 us (9%)
  other arithmetic  2.72 us (3%)
  local copies, waits for them, and re-layouts  1.6 us (2%)
  between operations  1.58 us (2%)
  matrix products  1.41 us (2%)
    ppermute x3, starting transfers between devices, per_device(): lax.ppermute(total, 'gy', partners('gy', 1, mask)).astype(f32)  17.8 us
    pallas_call x1, Pallas kernels, layer_call(): pl.pallas_call(functools.partial(layer_kernel, halo), out_shape=(jax.Shap...  17.7 us
    ppermute x8, starting transfers between devices, pair_exchange(): return (lax.ppermute(to_far, axis, far), lax.ppermute(to_near, axis, near))  13.7 us
    ppermute x3, starting transfers between devices, per_device(): lax.ppermute(piece, 'gx', partners('gx', stride, mask)).astype(f32)  13.1 us
    ppermute x3, starting transfers between devices, per_device(): piece = lax.ppermute(total, 'gx', partners('gx', stride, mask))  4.04 us
    ppermute x8, waiting for transfers between devices, pair_exchange(): return (lax.ppermute(to_far, axis, far), lax.ppermute(to_near, axis, near))  3.65 us
    ppermute x1, starting transfers between devices, per_device(): got = lax.ppermute(grads_send, 'gx', partners('gx', 1, 1))  3.48 us
    ppermute x3, waiting for transfers between devices, per_device(): lax.ppermute(piece, 'gx', partners('gx', stride, mask)).astype(f32)  2.53 us
  transfers between devices with their start and end apart: 19, of which 7 were waited for; matrix products, arithmetic and copies ran while one was open for 3% of the time, Pallas kernels for 0%

profile of v1, /device:TPU:0, one launch (start us, length us, event | category | flops | bytes accessed | tf_op | source)
XLA Modules:
  0.0 86.7 jit_solution(15925303007744214847)
XLA Ops:
  0.6 1.0 %convolution_convert_fusion = bf16[64,128]{1,0:T(8,128)(2,1)S(1)} fusion(bf16[256,128]{1,0:T(8,128)(2,1)} %latents_ref.1, s32[64]{0:T(128)} %bitcast.13), kind=kOutput, calls=%fused_computation | convolution fusion | flops 4218880 | bytes 82176 | tf_op jit(solution)/shard_map/dot_general | solution.py:713
  3.1 3.0 %collective-permute-start.3 = (bf16[192,128]{1,0:T(8,128)(2,1)S(1)}, bf16[192,128]{1,0:T(8,128)(2,1)S(1)}, u32[]{:S(2)}, u32[]{:S(2)}) collective-permute-start(bf16[192,128]{1,0:T(8,128)(2,1)S(1)} %pad_maximum_fusion.ring_ref), channel_id=1, source_target_pairs={{0,1},{1,0},{2,3},{3,2},{4,5},{5,4},{6,7},{7,6},{8,9},{9,8},{10,11... | collective-permute-start | bytes 147464 | tf_op jit(solution)/shard_map/ppermute | solution.py:684
  6.1 0.7 collective-permute-start.2
  7.4 0.8 collective-permute-done.3.ring_near_ref
  8.8 17.7 %edge_layer.1 = (bf16[256,128]{1,0:T(8,128)(2,1)}, bf16[1024,16,128]{2,1,0:T(8,128)(2,1)}, bf16[1024,16,128]{2,1,0:T(8,128)(2,1)}, f32[256,128]{1,0:T(8,128)}, b...) custom-call(s32[1]{0:T(128)S(6)} %copy.35.count_ref, ...), custom_call_target="tpu_custom_call" | custom-call | tf_op jit(solution)/shard_map/edge_layer/pallas_call | solution.py:525
  26.6 3.5 %collective-permute-start.4 = (bf16[640,128]{1,0:T(8,128)(2,1)}, bf16[640,128]{1,0:T(8,128)(2,1)S(1)}, u32[]{:S(2)}, u32[]{:S(2)}) collective-permute-start(bf16[640,128]{1,0:T(8,128)(2,1)} %get-tuple-element.45), channel_id=1, source_target_pairs={{0,4},{4,0},{8,12},{12,8},{16,20},{20,16},{24,28},{28,24},{1,5},{5... | collective-permute-start | bytes 491528 | tf_op jit(solution)/shard_map/ppermute | solution.py:734
  30.0 1.2 %collective-permute-done.4 = bf16[640,128]{1,0:T(8,128)(2,1)S(1)} collective-permute-done((bf16[640,128]{1,0:T(8,128)(2,1)}, bf16[640,128]{1,0:T(8,128)(2,1)S(1)}, u32[]{:S(2)}, u32[]{:S(2)}) %collective-permute-start.4) | collective-permute-done | bytes 163872 | tf_op jit(solution)/shard_map/ppermute | solution.py:734
  31.3 1.0 %add_convert_fusion = bf16[640,128]{1,0:T(8,128)(2,1)S(1)} fusion(f32[640,128]{1,0:T(8,128)} %get-tuple-element.44, bf16[640,128]{1,0:T(8,128)(2,1)S(1)} %collective-permute-done.4), kind=kLoop, calls=%fused_computation.1 | loop fusion | flops 245760 | bytes 655360 | tf_op jit(solution)/shard_map/convert_element_type | solution.py:735
  32.3 9.0 %collective-permute-start.5 = (bf16[160,128]{1,0:T(8,128)(2,1)S(1)}, bf16[160,128]{1,0:T(8,128)(2,1)S(1)}, u32[]{:S(2)}, u32[]{:S(2)}) collective-permute-start(bf16[160,128]{1,0:T(8,128)(2,1)S(1)} %get-tuple-element.69), channel_id=1, source_target_pairs={{0,24},{4,28},{8,16},{12,20},{16,8},{20,12},{24,0},{28,4},{1,25},{... | collective-permute-start | bytes 122888 | tf_op jit(solution)/shard_map/ppermute | solution.py:743
  41.3 2.7 %collective-permute-start.7 = (bf16[160,128]{1,0:T(8,128)(2,1)S(1)}, bf16[160,128]{1,0:T(8,128)(2,1)S(1)}, u32[]{:S(2)}, u32[]{:S(2)}) collective-permute-start(bf16[160,128]{1,0:T(8,128)(2,1)S(1)} %get-tuple-element.70), channel_id=1, source_target_pairs={{0,8},{4,12},{8,0},{12,4},{16,24},{20,28},{24,16},{28,20},{1,9},{5... | collective-permute-start | bytes 122888 | tf_op jit(solution)/shard_map/ppermute | solution.py:743
  44.0 1.4 %collective-permute-start.6 = (bf16[160,128]{1,0:T(8,128)(2,1)S(1)}, bf16[160,128]{1,0:T(8,128)(2,1)S(1)}, u32[]{:S(2)}, u32[]{:S(2)}) collective-permute-start(bf16[160,128]{1,0:T(8,128)(2,1)S(1)} %get-tuple-element.71), channel_id=1, source_target_pairs={{0,16},{4,20},{8,24},{12,28},{16,0},{20,4},{24,8},{28,12},{1,17},{... | collective-permute-start | bytes 122888 | tf_op jit(solution)/shard_map/ppermute | solution.py:743
  45.5 1.4 %collective-permute-done.7 = bf16[160,128]{1,0:T(8,128)(2,1)S(1)} collective-permute-done((bf16[160,128]{1,0:T(8,128)(2,1)S(1)}, bf16[160,128]{1,0:T(8,128)(2,1)S(1)}, u32[]{:S(2)}, u32[]{:S(2)}) %collective-permute-start.7) | collective-permute-done | bytes 40992 | tf_op jit(solution)/shard_map/ppermute | solution.py:743
  46.9 1.1 %collective-permute-done.6 = bf16[160,128]{1,0:T(8,128)(2,1)S(1)} collective-permute-done((bf16[160,128]{1,0:T(8,128)(2,1)S(1)}, bf16[160,128]{1,0:T(8,128)(2,1)S(1)}, u32[]{:S(2)}, u32[]{:S(2)}) %collective-permute-start.6) | collective-permute-done | bytes 40992 | tf_op jit(solution)/shard_map/ppermute | solution.py:743
  48.0 17.1 %collective-permute-start.12 = (bf16[160,128]{1,0:T(8,128)(2,1)S(1)}, bf16[160,128]{1,0:T(8,128)(2,1)S(1)}, u32[]{:S(2)}, u32[]{:S(2)}) collective-permute-start(bf16[160,128]{1,0:T(8,128)(2,1)S(1)} %add_convert_fusion.3), channel_id=1, source_target_pairs={{0,3},{1,2},{2,1},{3,0},{4,7},{5,6},{6,5},{7,4},{8,11},{9,10},{10,... | collective-permute-start | bytes 122888 | tf_op jit(solution)/shard_map/ppermute | solution.py:748
  65.8 0.7 fusion.9
  66.5 0.7 collective-permute-start.8
  67.2 3.4 %collective-permute-start.9 = (bf16[192,128]{1,0:T(8,128)(2,1)}, bf16[192,128]{1,0:T(8,128)(2,1)S(1)}, u32[]{:S(2)}, u32[]{:S(2)}) collective-permute-start(bf16[192,128]{1,0:T(8,128)(2,1)} %get-tuple-element.49), channel_id=1, source_target_pairs={{0,4},{4,0},{8,12},{12,8},{16,20},{20,16},{24,28},{28,24},{1,5},{5... | collective-permute-start | bytes 147464 | tf_op jit(solution)/shard_map/ppermute | solution.py:684
  70.7 1.0 %collective-permute-done.9 = bf16[192,128]{1,0:T(8,128)(2,1)S(1)} collective-permute-done((bf16[192,128]{1,0:T(8,128)(2,1)}, bf16[192,128]{1,0:T(8,128)(2,1)S(1)}, u32[]{:S(2)}, u32[]{:S(2)}) %collective-permute-start.9) | collective-permute-done | bytes 49184 | tf_op jit(solution)/shard_map/ppermute | solution.py:684
  71.9 2.5 %collective-permute-start.17 = (bf16[160,128]{1,0:T(8,128)(2,1)S(1)}, bf16[160,128]{1,0:T(8,128)(2,1)S(1)}, u32[]{:S(2)}, u32[]{:S(2)}) collective-permute-start(bf16[160,128]{1,0:T(8,128)(2,1)S(1)} %add_convert_fusion.2), channel_id=1, source_target_pairs={{0,8},{4,12},{8,0},{12,4},{16,24},{20,28},{24,16},{28,20},{1,9},{5... | collective-permute-start | bytes 122888 | tf_op jit(solution)/shard_map/ppermute | solution.py:770
  74.8 1.1 %collective-permute-start.15 = (bf16[160,128]{1,0:T(8,128)(2,1)S(1)}, bf16[160,128]{1,0:T(8,128)(2,1)S(1)}, u32[]{:S(2)}, u32[]{:S(2)}) collective-permute-start(bf16[160,128]{1,0:T(8,128)(2,1)S(1)} %add_convert_fusion.2), channel_id=1, source_target_pairs={{0,24},{4,28},{8,16},{12,20},{16,8},{20,12},{24,0},{28,4},{1,25},{... | collective-permute-start | bytes 122888 | tf_op jit(solution)/shard_map/ppermute | solution.py:770
  76.6 4.2 %collective-permute-start.14 = (bf16[64,128]{1,0:T(8,128)(2,1)S(1)}, bf16[64,128]{1,0:T(8,128)(2,1)S(1)}, u32[]{:S(2)}, u32[]{:S(2)}) collective-permute-start(bf16[64,128]{1,0:T(8,128)(2,1)S(1)} %get-tuple-element.75), channel_id=1, source_target_pairs={{0,1},{1,0},{2,3},{3,2},{4,5},{5,4},{6,7},{7,6},{8,9},{9,8},{10,11... | collective-permute-start | bytes 49160 | tf_op jit(solution)/shard_map/ppermute | solution.py:684
  80.8 1.7 %collective-permute-done.14 = bf16[64,128]{1,0:T(8,128)(2,1)S(1)} collective-permute-done((bf16[64,128]{1,0:T(8,128)(2,1)S(1)}, bf16[64,128]{1,0:T(8,128)(2,1)S(1)}, u32[]{:S(2)}, u32[]{:S(2)}) %collective-permute-start.14) | collective-permute-done | bytes 16416 | tf_op jit(solution)/shard_map/ppermute | solution.py:684
  83.0 1.6 %add_convert_fusion.1 = bf16[256,128]{1,0:T(8,128)(2,1)} fusion(f32[256,128]{1,0:T(8,128)} %get-tuple-element.43, f32[256,128]{1,0:T(8,128)S(1)} %fusion), kind=kLoop, calls=%fused_computation.2 | loop fusion | flops 65536 | bytes 327680 | tf_op jit(solution)/shard_map/convert_element_type | solution.py:782
  84.6 2.0 %update.1 = (f32[1,1]{1,0:T(1,128)}, f32[9,128,128]{2,1,0:T(8,128)}, f32[10,128]{1,0:T(8,128)}, f32[9,128,128]{2,1,0:T(8,128)}, f32[10,128]{1,0:T(8,128)}, /*ind...) custom-call(bf16[640,128]{1,0:T(8,128)(2,1)S(1)} %constant_dynamic-u, ...), custom_call_target="tpu_custom_call" | custom-call | tf_op jit(solution)/shard_map/update/pallas_call | solution.py:670
  (59 shorter events, 4.5 us)
Async XLA Ops:
  1.7 1.4 %collective-permute-start.1 = (bf16[64,128]{1,0:T(8,128)(2,1)S(1)}, bf16[64,128]{1,0:T(8,128)(2,1)S(1)}, u32[]{:S(2)}, u32[]{:S(2)}) collective-permute-start(bf16[64,128]{1,0:T(8,128)(2,1)S(1)} %convolution_convert_fusion), channel_id=1, source_target_pairs={{0,4},{4,0},{8,12},{12,8},{16,20},{20,16},{24,28},{28,24},{1,5},{5... | collective-permute-start | bytes 49160 | tf_op jit(solution)/shard_map/ppermute | solution.py:684
  2.2 0.8 collective-permute-start
  3.1 5.1 %collective-permute-start.3 = (bf16[192,128]{1,0:T(8,128)(2,1)S(1)}, bf16[192,128]{1,0:T(8,128)(2,1)S(1)}, u32[]{:S(2)}, u32[]{:S(2)}) collective-permute-start(bf16[192,128]{1,0:T(8,128)(2,1)S(1)} %pad_maximum_fusion.ring_ref), channel_id=1, source_target_pairs={{0,1},{1,0},{2,3},{3,2},{4,5},{5,4},{6,7},{7,6},{8,9},{9,8},{10,11... | collective-permute-start | bytes 147464 | tf_op jit(solution)/shard_map/ppermute | solution.py:684
  6.1 2.1 %collective-permute-start.2 = (bf16[192,128]{1,0:T(8,128)(2,1)S(1)}, bf16[192,128]{1,0:T(8,128)(2,1)S(1)}, u32[]{:S(2)}, u32[]{:S(2)}) collective-permute-start(bf16[192,128]{1,0:T(8,128)(2,1)S(1)} %pad_maximum_fusion.ring_ref), channel_id=1, source_target_pairs={{1,2},{2,1},{5,6},{6,5},{9,10},{10,9},{13,14},{14,13},{17,18},{18,... | collective-permute-start | bytes 147464 | tf_op jit(solution)/shard_map/ppermute | solution.py:684
  8.8 75.8 %copy-start.2 = (f32[9,128,128]{2,1,0:T(8,128)S(1)}, f32[9,128,128]{2,1,0:T(8,128)}, u32[]{:S(2)}) copy-start(f32[9,128,128]{2,1,0:T(8,128)} %weights_v_ref.1) | copy-start | bytes 1769476
  8.8 75.8 %copy-start.3 = (f32[9,128,128]{2,1,0:T(8,128)S(1)}, f32[9,128,128]{2,1,0:T(8,128)}, u32[]{:S(2)}) copy-start(f32[9,128,128]{2,1,0:T(8,128)} %weights_ema_ref.1) | copy-start | bytes 1769476
  8.8 75.8 %copy-start.4 = (f32[10,128]{1,0:T(8,128)S(1)}, f32[10,128]{1,0:T(8,128)}, u32[]{:S(2)}) copy-start(f32[10,128]{1,0:T(8,128)} %vectors_ref.3) | copy-start | bytes 15364
  8.8 75.8 %copy-start.5 = (f32[10,128]{1,0:T(8,128)S(1)}, f32[10,128]{1,0:T(8,128)}, u32[]{:S(2)}) copy-start(f32[10,128]{1,0:T(8,128)} %vectors_m_ref.1) | copy-start | bytes 15364
  8.8 75.8 %copy-start.6 = (f32[10,128]{1,0:T(8,128)S(1)}, f32[10,128]{1,0:T(8,128)}, u32[]{:S(2)}) copy-start(f32[10,128]{1,0:T(8,128)} %vectors_v_ref.1) | copy-start | bytes 15364
  26.6 4.7 %collective-permute-start.4 = (bf16[640,128]{1,0:T(8,128)(2,1)}, bf16[640,128]{1,0:T(8,128)(2,1)S(1)}, u32[]{:S(2)}, u32[]{:S(2)}) collective-permute-start(bf16[640,128]{1,0:T(8,128)(2,1)} %get-tuple-element.45), channel_id=1, source_target_pairs={{0,4},{4,0},{8,12},{12,8},{16,20},{20,16},{24,28},{28,24},{1,5},{5... | collective-permute-start | bytes 491528 | tf_op jit(solution)/shard_map/ppermute | solution.py:734
  32.3 13.2 %collective-permute-start.5 = (bf16[160,128]{1,0:T(8,128)(2,1)S(1)}, bf16[160,128]{1,0:T(8,128)(2,1)S(1)}, u32[]{:S(2)}, u32[]{:S(2)}) collective-permute-start(bf16[160,128]{1,0:T(8,128)(2,1)S(1)} %get-tuple-element.69), channel_id=1, source_target_pairs={{0,24},{4,28},{8,16},{12,20},{16,8},{20,12},{24,0},{28,4},{1,25},{... | collective-permute-start | bytes 122888 | tf_op jit(solution)/shard_map/ppermute | solution.py:743
  41.3 5.6 %collective-permute-start.7 = (bf16[160,128]{1,0:T(8,128)(2,1)S(1)}, bf16[160,128]{1,0:T(8,128)(2,1)S(1)}, u32[]{:S(2)}, u32[]{:S(2)}) collective-permute-start(bf16[160,128]{1,0:T(8,128)(2,1)S(1)} %get-tuple-element.70), channel_id=1, source_target_pairs={{0,8},{4,12},{8,0},{12,4},{16,24},{20,28},{24,16},{28,20},{1,9},{5... | collective-permute-start | bytes 122888 | tf_op jit(solution)/shard_map/ppermute | solution.py:743
  44.0 4.0 %collective-permute-start.6 = (bf16[160,128]{1,0:T(8,128)(2,1)S(1)}, bf16[160,128]{1,0:T(8,128)(2,1)S(1)}, u32[]{:S(2)}, u32[]{:S(2)}) collective-permute-start(bf16[160,128]{1,0:T(8,128)(2,1)S(1)} %get-tuple-element.71), channel_id=1, source_target_pairs={{0,16},{4,20},{8,24},{12,28},{16,0},{20,4},{24,8},{28,12},{1,17},{... | collective-permute-start | bytes 122888 | tf_op jit(solution)/shard_map/ppermute | solution.py:743
  48.0 22.6 %collective-permute-start.12 = (bf16[160,128]{1,0:T(8,128)(2,1)S(1)}, bf16[160,128]{1,0:T(8,128)(2,1)S(1)}, u32[]{:S(2)}, u32[]{:S(2)}) collective-permute-start(bf16[160,128]{1,0:T(8,128)(2,1)S(1)} %add_convert_fusion.3), channel_id=1, source_target_pairs={{0,3},{1,2},{2,1},{3,0},{4,7},{5,6},{6,5},{7,4},{8,11},{9,10},{10,... | collective-permute-start | bytes 122888 | tf_op jit(solution)/shard_map/ppermute | solution.py:748
  65.2 5.5 %collective-permute-start.11 = (bf16[160,128]{1,0:T(8,128)(2,1)S(1)}, bf16[160,128]{1,0:T(8,128)(2,1)S(1)}, u32[]{:S(2)}, u32[]{:S(2)}) collective-permute-start(bf16[160,128]{1,0:T(8,128)(2,1)S(1)} %add_convert_fusion.3), channel_id=1, source_target_pairs={{0,2},{1,3},{2,0},{3,1},{4,6},{5,7},{6,4},{7,5},{8,10},{9,11},{10,... | collective-permute-start | bytes 122888 | tf_op jit(solution)/shard_map/ppermute | solution.py:748
  65.2 5.5 %collective-permute-start.10 = (bf16[160,128]{1,0:T(8,128)(2,1)S(1)}, bf16[160,128]{1,0:T(8,128)(2,1)S(1)}, u32[]{:S(2)}, u32[]{:S(2)}) collective-permute-start(bf16[160,128]{1,0:T(8,128)(2,1)S(1)} %add_convert_fusion.3), channel_id=1, source_target_pairs={{0,1},{1,0},{2,3},{3,2},{4,5},{5,4},{6,7},{7,6},{8,9},{9,8},{10,11... | collective-permute-start | bytes 122888 | tf_op jit(solution)/shard_map/ppermute | solution.py:748
  66.5 4.2 %collective-permute-start.8 = (bf16[192,128]{1,0:T(8,128)(2,1)}, bf16[192,128]{1,0:T(8,128)(2,1)S(1)}, u32[]{:S(2)}, u32[]{:S(2)}) collective-permute-start(bf16[192,128]{1,0:T(8,128)(2,1)} %get-tuple-element.48), channel_id=1, source_target_pairs={{4,8},{12,16},{20,24},{8,4},{16,12},{24,20},{5,9},{13,17},{21,25},... | collective-permute-start | bytes 147464 | tf_op jit(solution)/shard_map/ppermute | solution.py:684
  67.2 4.5 %collective-permute-start.9 = (bf16[192,128]{1,0:T(8,128)(2,1)}, bf16[192,128]{1,0:T(8,128)(2,1)S(1)}, u32[]{:S(2)}, u32[]{:S(2)}) collective-permute-start(bf16[192,128]{1,0:T(8,128)(2,1)} %get-tuple-element.49), channel_id=1, source_target_pairs={{0,4},{4,0},{8,12},{12,8},{16,20},{20,16},{24,28},{28,24},{1,5},{5... | collective-permute-start | bytes 147464 | tf_op jit(solution)/shard_map/ppermute | solution.py:684
  71.9 11.0 %collective-permute-start.17 = (bf16[160,128]{1,0:T(8,128)(2,1)S(1)}, bf16[160,128]{1,0:T(8,128)(2,1)S(1)}, u32[]{:S(2)}, u32[]{:S(2)}) collective-permute-start(bf16[160,128]{1,0:T(8,128)(2,1)S(1)} %add_convert_fusion.2), channel_id=1, source_target_pairs={{0,8},{4,12},{8,0},{12,4},{16,24},{20,28},{24,16},{28,20},{1,9},{5... | collective-permute-start | bytes 122888 | tf_op jit(solution)/shard_map/ppermute | solution.py:770
  74.4 8.5 %collective-permute-start.16 = (bf16[160,128]{1,0:T(8,128)(2,1)S(1)}, bf16[160,128]{1,0:T(8,128)(2,1)S(1)}, u32[]{:S(2)}, u32[]{:S(2)}) collective-permute-start(bf16[160,128]{1,0:T(8,128)(2,1)S(1)} %add_convert_fusion.2), channel_id=1, source_target_pairs={{0,16},{4,20},{8,24},{12,28},{16,0},{20,4},{24,8},{28,12},{1,17},{... | collective-permute-start | bytes 122888 | tf_op jit(solution)/shard_map/ppermute | solution.py:770
  74.8 8.1 %collective-permute-start.15 = (bf16[160,128]{1,0:T(8,128)(2,1)S(1)}, bf16[160,128]{1,0:T(8,128)(2,1)S(1)}, u32[]{:S(2)}, u32[]{:S(2)}) collective-permute-start(bf16[160,128]{1,0:T(8,128)(2,1)S(1)} %add_convert_fusion.2), channel_id=1, source_target_pairs={{0,24},{4,28},{8,16},{12,20},{16,8},{20,12},{24,0},{28,4},{1,25},{... | collective-permute-start | bytes 122888 | tf_op jit(solution)/shard_map/ppermute | solution.py:770
  75.9 4.9 %collective-permute-start.13 = (bf16[64,128]{1,0:T(8,128)(2,1)S(1)}, bf16[64,128]{1,0:T(8,128)(2,1)S(1)}, u32[]{:S(2)}, u32[]{:S(2)}) collective-permute-start(bf16[64,128]{1,0:T(8,128)(2,1)S(1)} %get-tuple-element.74), channel_id=1, source_target_pairs={{1,2},{2,1},{5,6},{6,5},{9,10},{10,9},{13,14},{14,13},{17,18},{18,... | collective-permute-start | bytes 49160 | tf_op jit(solution)/shard_map/ppermute | solution.py:684
  76.6 5.9 %collective-permute-start.14 = (bf16[64,128]{1,0:T(8,128)(2,1)S(1)}, bf16[64,128]{1,0:T(8,128)(2,1)S(1)}, u32[]{:S(2)}, u32[]{:S(2)}) collective-permute-start(bf16[64,128]{1,0:T(8,128)(2,1)S(1)} %get-tuple-element.75), channel_id=1, source_target_pairs={{0,1},{1,0},{2,3},{3,2},{4,5},{5,4},{6,7},{7,6},{8,9},{9,8},{10,11... | collective-permute-start | bytes 49160 | tf_op jit(solution)/shard_map/ppermute | solution.py:684
  82.9 1.6 %collective-permute-start.18 = (bf16[640,128]{1,0:T(8,128)(2,1)S(1)}, bf16[640,128]{1,0:T(8,128)(2,1)S(1)}, u32[]{:S(2)}, u32[]{:S(2)}) collective-permute-start(bf16[640,128]{1,0:T(8,128)(2,1)S(1)} %constant_dynamic-update-slice_fusion.mine_ref), channel_id=1, source_target_pairs={{0,4},{4,0},{8,12},{12,8},{16,20},{20,16},{24,28},{28,24},{1,5},{5... | collective-permute-start | bytes 491528 | tf_op jit(solution)/shard_map/ppermute | solution.py:773
  (7 other events, 307.4 us)

commit v2 on v1

--- a/solution.py
+++ b/solution.py
@@ -116,8 +116,13 @@
     return lax.broadcasted_iota(jnp.int32, shape, dim)
 
 
+def slot_rows(quarter, halo):
+    return (0, quarter, 3 * quarter + 3 * halo, 2 * quarter + 3 * halo)
+
+
 def layer_kernel(
     halo,
+    relayed,
     count_ref,
     neighbour_ref,
     mask_ref,
@@ -134,11 +139,9 @@
     edges_out_hbm,
     edges_grad_hbm,
     node_part_ref,
-    halo_far_ref,
-    halo_near_ref,
     halo_own_ref,
-    grads_send_ref,
-    grads_keep_ref,
+    send_ref,
+    keep_ref,
     edges_buf,
     cotangent_buf,
     kept_edges,
@@ -165,6 +168,8 @@
     vec_acc,
     first_tile,
     third_tile,
+    first_back,
+    second_back,
     passed_tile,
     halo_grad,
     grads,
@@ -339,6 +344,8 @@
             )
             receiver_tile[j : j + 1, :] = receiver_ref[pl.ds(particle, 1), :]
         gather_ref[rows + width : rows + width + GROUP, :] = split_pair(receiver_tile[...])
+
+    def project(t):
         picks = jnp.concatenate(one_hot(t) + [flat(kept_edges, t), blocks_ref[0]], axis=1)
         first_tile[...] = halves(dot(picks, gather_ref[...]))
 
@@ -346,16 +353,18 @@
 
     def forward(t, carry):
         base = t * GROUP
+        gather(t + 1)
         act, slope = silu_of_half(first_tile[...])
         act = act.astype(bf16)
         keep(kept_act1, t, act)
         keep(kept_slope1, t, slope)
-        gather(t + 1)
         act, slope = silu_of_half(dot(act, half3) + 0.5 * vector(1))
         act = act.astype(bf16)
         keep(kept_act2, t, act)
         keep(kept_slope2, t, slope)
-        unit, inverse = scaled_unit(dot(act, low_ref[4]) + vector(2), width)
+        last = dot(act, low_ref[4]) + vector(2)
+        project(t + 1)
+        unit, inverse = scaled_unit(last, width)
         keep(kept_unit, t, unit)
         keep(kept_inverse, t, jnp.broadcast_to(inverse, (TILE, width)))
         change = unit * gain_root + vector(4)
@@ -368,8 +377,10 @@
         return carry
 
     gather(0)
+    project(0)
     lax.fori_loop(0, tiles, forward, 0)
-    keep(kept_unit, tiles, jnp.zeros((TILE, width), f32))
+    for ref in (kept_act1, kept_unit, kept_inverse):
+        keep(ref, tiles, jnp.zeros((TILE, width), f32))
 
     stores = [
         pltpu.make_async_copy(
@@ -419,7 +430,7 @@
     def add_columns(row, values):
         vec_acc[8 * row : 8 * row + 8, :] += jnp.sum(values.reshape(TILE // 8, 8, width), axis=0)
 
-    def descend(t):
+    def accept(t):
         base = t * GROUP
         parts = []
         for j in range(GROUP):
@@ -428,39 +439,48 @@
             passed = cotangent_buf[chunk].astype(f32) + jnp.where(
                 alive, receiver_ref[pl.ds(particle, 1), :], 0.0
             )
-            passed_tile[t & 1, span(j), :] = passed
+            passed_tile[t & 3, span(j), :] = passed
             parts.append(jnp.where(alive, passed, 0.0))
-        held = jnp.concatenate(parts, axis=0)
+        return jnp.concatenate(parts, axis=0)
+
+    def descend(t, held):
         unit = flat(kept_unit, t).astype(f32)
         third = scaled_unit_back(held * gain_root, unit, flat(kept_inverse, t), width)
         third_tile[...] = third.astype(bf16)
-        return held, unit, third
-
-    def backward(t, carry):
-        base = t * GROUP
-        third = third_tile[...]
-        third_f32 = third.astype(f32)
-        second = 1.0 * flat(kept_slope2, t).astype(f32) * dot_nt(third, half4)
-        add_columns(1, second)
-        add_columns(2, third_f32)
-        second = second.astype(bf16)
-        mat_acc[1] += dot_tn(flat(kept_act2, t), third)
-        held, unit, _ = descend(t + 1)
+        add_columns(2, third)
         add_columns(3, held * unit)
         add_columns(4, held)
-        first = (flat(kept_slope1, t).astype(f32) * dot_nt(second, half3)).astype(bf16)
-        result = passed_tile[t & 1] + dot_nt(first, low_ref[0])
+
+    def settle(t, slot):
+        base = t * GROUP
+        first = first_back[...]
+        result = passed_tile[slot] + dot_nt(first, low_ref[0])
         for j in range(GROUP):
             cotangent_buf[listed[0, base + j]] = result[span(j)].astype(bf16)
-        mat_acc[0] += dot_tn(flat(kept_act1, t), second)
         picks = jnp.concatenate(one_hot(t) + [flat(kept_edges, t), blocks_ref[t & 3]], axis=1)
         index_acc[...] += dot_tn(first, picks[:, 0 : rows + width])
         chunk_grads[t >> 2] += dot_tn(first, picks[:, rows + width :])
+        mat_acc[0] += dot_tn(flat(kept_act1, t), second_back[...])
+
+    def backward(t, carry):
+        third = third_tile[...]
+        second = dot_nt(third, half4)
+        held = accept(t + 1)
+        settle(jnp.where(t == 0, tiles, t - 1), (t + 3) & 3)
+        second = flat(kept_slope2, t).astype(f32) * second
+        add_columns(1, second)
+        second = second.astype(bf16)
+        descend(t + 1, held)
+        first = flat(kept_slope1, t).astype(f32) * dot_nt(second, half3)
+        mat_acc[1] += dot_tn(flat(kept_act2, t), third)
+        first_back[...] = first.astype(bf16)
+        second_back[...] = second
         return carry
 
-    held, unit, _ = descend(0)
-    add_columns(3, held * unit)
-    add_columns(4, held)
+    first_back[...] = jnp.zeros(first_back.shape, bf16)
+    second_back[...] = jnp.zeros(second_back.shape, bf16)
+    passed_tile[3] = jnp.zeros((TILE, width), f32)
+    descend(0, accept(0))
     results = [
         pltpu.make_async_copy(
             cotangent_buf.at[pl.ds(p * piece, piece)],
@@ -470,11 +490,12 @@
         for p in range(PIECES)
     ]
     lax.fori_loop(0, tiles, backward, 0)
+    settle(jnp.where(tiles == 0, tiles, tiles - 1), (tiles + 3) & 3)
     for copy in results:
         copy.start()
 
     stacked = split_pair(
-        jnp.concatenate([chunk_grads[g] for g in range(chunk_grads.shape[0])], axis=1), axis=0
+        jnp.concatenate([chunk_grads[g] for g in range(chunks // LANES)], axis=1), axis=0
     )
     receiver_grad = halves(dot_nt(segment_ref[...], stacked)).astype(bf16)
     grads[tail : tail + 1, :] = halves(dot_nt(jnp.ones((8, chunks), bf16), stacked))[0:1, :]
@@ -494,20 +515,28 @@
     halo_grad[...] = table_grad[particles:, :].astype(bf16)
     low_x = halo_grad[0 : 3 * halo, :]
     high_x = halo_grad[5 * halo : 8 * halo, :]
-    halo_far_ref[...] = jnp.where(odd_x == 0, low_x, high_x)
-    halo_near_ref[...] = jnp.where(odd_x == 0, high_x, low_x)
-    halo_own_ref[...] = halo_grad[3 * halo : 5 * halo, :]
-    part_rows = grads_keep_ref.shape[0]
-    lower, upper = grads[0:part_rows, :], grads[part_rows:, :]
-    grads_keep_ref[...] = jnp.where(odd_x == 0, lower, upper)
-    grads_send_ref[...] = jnp.where(odd_x == 0, upper, lower).astype(bf16)
+    halo_own_ref[0:halo, :] = halo_grad[3 * halo : 4 * halo, :]
+    halo_own_ref[halo : 2 * halo, :] = jnp.zeros((halo, width), bf16)
+    halo_own_ref[2 * halo :, :] = halo_grad[4 * halo : 5 * halo, :]
+    quarter = grads.shape[0] // 8
+    order = (lax.axis_index("gx") >> 1) & 3 if relayed else 0
+    relay = 2 * quarter
+    send_ref[relay : relay + 3 * halo, :] = jnp.where(odd_x == 0, low_x, high_x)
+    send_ref[relay + 2 * quarter + 3 * halo :, :] = jnp.where(odd_x == 0, high_x, low_x)
+    keep_ref[relay : relay + 3 * halo, :] = jnp.zeros((3 * halo, width), f32)
+    for slot, spot in enumerate(slot_rows(quarter, halo)):
+        inner = (slot ^ order) * quarter
+        kept_rows = pl.ds(pl.multiple_of(odd_x * 4 * quarter + inner, 16), quarter)
+        sent_rows = pl.ds(pl.multiple_of((1 - odd_x) * 4 * quarter + inner, 16), quarter)
+        keep_ref[spot : spot + quarter, :] = grads[kept_rows, :]
+        send_ref[spot : spot + quarter, :] = grads[sent_rows, :].astype(bf16)
 
     for copy in stores + results:
         copy.wait()
 
 
 def layer_call(
-    halo, grad_rows, counts, neighbours, edge_mask, latents, ring, ring_far, ring_near, upstream,
+    halo, relayed, grad_rows, counts, neighbours, edge_mask, latents, ring, ring_far, ring_near, upstream,
     vectors, weights, edges, cotangents,
 ):
     f32, bf16, i32 = jnp.float32, jnp.bfloat16, jnp.int32
@@ -521,22 +550,20 @@
     kept_shape = (chunks + GROUP, CHUNK, width)
     kept = pltpu.VMEM(kept_shape, bf16)
     buffer = pltpu.VMEM((chunks + 1, CHUNK, width), bf16)
-    strip = jax.ShapeDtypeStruct((3 * halo, width), bf16)
+    half = grad_rows // 2
     return pl.pallas_call(
-        functools.partial(layer_kernel, halo),
+        functools.partial(layer_kernel, halo, relayed),
         out_shape=(
             jax.ShapeDtypeStruct((particles, width), bf16),
             jax.ShapeDtypeStruct(edge_shape, bf16),
             jax.ShapeDtypeStruct(edge_shape, bf16),
             jax.ShapeDtypeStruct((particles, width), f32),
-            strip,
-            strip,
-            jax.ShapeDtypeStruct((2 * halo, width), bf16),
-            jax.ShapeDtypeStruct((grad_rows // 2, width), bf16),
-            jax.ShapeDtypeStruct((grad_rows // 2, width), f32),
+            jax.ShapeDtypeStruct((3 * halo, width), bf16),
+            jax.ShapeDtypeStruct((half + 6 * halo, width), bf16),
+            jax.ShapeDtypeStruct((half + 3 * halo, width), f32),
         ),
         in_specs=[pl.BlockSpec(memory_space=pltpu.SMEM)] + [whole] * 8 + [outside] * 3,
-        out_specs=(whole, outside, outside, whole, whole, whole, whole, whole, whole),
+        out_specs=(whole, outside, outside, whole, whole, whole, whole),
         scratch_shapes=[
             buffer,
             buffer,
@@ -558,13 +585,15 @@
             pltpu.VMEM((particles, chunks), bf16),
             pltpu.VMEM((LANES // GROUP, TILE, LANES), bf16),
             pltpu.VMEM((chunks, width), f32),
-            pltpu.VMEM((chunks // LANES, width, LANES), f32),
+            pltpu.VMEM((chunks // LANES + 1, width, LANES), f32),
             pltpu.VMEM((width, rows + width), f32),
             pltpu.VMEM((2, width, width), f32),
             pltpu.VMEM((40, width), f32),
             pltpu.VMEM((TILE, width), f32),
             pltpu.VMEM((TILE, width), bf16),
-            pltpu.VMEM((2, TILE, width), f32),
+            pltpu.VMEM((TILE, width), bf16),
+            pltpu.VMEM((TILE, width), bf16),
+            pltpu.VMEM((4, TILE, width), f32),
             pltpu.VMEM((8 * halo, width), bf16),
             pltpu.VMEM((grad_rows, width), f32),
             pltpu.VMEM((8, chunks + LANES), i32),
@@ -593,8 +622,11 @@
 
 
 def update_kernel(
-    mine_ref,
-    other_ref,
+    relayed,
+    part0_ref,
+    part1_ref,
+    part2_ref,
+    part3_ref,
     weights_ref,
     vectors_ref,
     weights_m_ref,
@@ -618,11 +650,17 @@
 ):
     f32 = jnp.float32
     odd = lax.axis_index("gx") & 1
-    part_rows, width = mine_ref.shape
-    mine, other = mine_ref[...].astype(f32), other_ref[...].astype(f32)
-    grads[0:part_rows, :] = jnp.where(odd == 0, mine, other)
-    grads[part_rows:, :] = jnp.where(odd == 0, other, mine)
-    squares = jnp.sum((mine * mine + other * other).reshape(part_rows // 8, 8, width), axis=0)
+    pair_rows, width = part0_ref.shape
+    quarter = pair_rows // 2
+    order = (lax.axis_index("gx") >> 1) & 3 if relayed else 0
+    squares = jnp.zeros((8, width), f32)
+    for slot, part_ref in enumerate((part0_ref, part1_ref, part2_ref, part3_ref)):
+        part = part_ref[...].astype(f32)
+        for side in range(2):
+            values = part[side * quarter : (side + 1) * quarter, :]
+            spot = ((odd ^ side) * 4 + (slot ^ order)) * quarter
+            grads[pl.ds(pl.multiple_of(spot, 16), quarter), :] = values
+            squares = squares + jnp.sum((values * values).reshape(quarter // 8, 8, width), axis=0)
     norm = jnp.sqrt(jnp.sum(jnp.sum(squares, axis=1, keepdims=True), axis=0, keepdims=True))
     norm_ref[...] = norm
     scale = clip_norm / jnp.maximum(norm, clip_norm)
@@ -658,7 +696,7 @@
     vectors_ema_out[...] = average
 
 
-def update_call(mine, other, weights, vectors, weights_m, vectors_m, weights_v, vectors_v,
+def update_call(relayed, parts, weights, vectors, weights_m, vectors_m, weights_v, vectors_v,
                 weights_ema, vectors_ema):
     f32, bf16 = jnp.float32, jnp.bfloat16
     mat, vec = weights.shape, vectors.shape
@@ -668,14 +706,14 @@
     )
     whole = pl.BlockSpec(memory_space=pltpu.VMEM)
     return pl.pallas_call(
-        update_kernel,
+        functools.partial(update_kernel, relayed),
         out_shape=tuple(jax.ShapeDtypeStruct(*kind) for kind in kinds),
-        in_specs=[whole] * 10,
+        in_specs=[whole] * 12,
         out_specs=(whole,) * 11,
-        scratch_shapes=[pltpu.VMEM((2 * mine.shape[0], mine.shape[1]), f32)],
+        scratch_shapes=[pltpu.VMEM((4 * parts[0].shape[0], parts[0].shape[1]), f32)],
         compiler_params=pltpu.CompilerParams(vmem_limit_bytes=24 * 1024 * 1024),
         name="update",
-    )(mine, other, weights, vectors, weights_m, vectors_m, weights_v, vectors_v, weights_ema,
+    )(*parts, weights, vectors, weights_m, vectors_m, weights_v, vectors_v, weights_ema,
       vectors_ema)
 
 
@@ -686,6 +724,112 @@
 
 def partners(axis, stride, mask):
     return [(i, i ^ (mask * stride)) for i in range(lax.axis_size(axis))]
+
+
+def even_pick(axis, even, odd):
+    return jnp.where(lax.axis_index(axis) % 2 == 0, even, odd)
+
+
+def swap(values, axis, stride, mask):
+    return lax.ppermute(values, axis, partners(axis, stride, mask))
+
+
+def tree_sum(terms):
+    while len(terms) > 1:
+        terms = [terms[i] + terms[i + 1] for i in range(0, len(terms), 2)]
+    return terms[0]
+
+
+def sum_relayed(send, keep, halo_own, halo):
+    f32, bf16 = jnp.float32, jnp.bfloat16
+    quarter = (send.shape[0] - 6 * halo) // 4
+    slots = slot_rows(quarter, halo)
+    index, row = lax.axis_index("gx"), lax.axis_index("gy")
+    got = swap(send, "gx", 1, 1)
+    near = got[4 * quarter + 3 * halo :].astype(f32)
+    total = (keep + got[: 4 * quarter + 3 * halo].astype(f32)).astype(bf16)
+    from3 = swap(total[2 * quarter : 3 * quarter + 3 * halo], "gx", 2, 3)
+    from2 = swap(total[slots[2] : slots[2] + quarter], "gx", 2, 2)
+    from1 = swap(total[quarter : 2 * quarter + 3 * halo], "gx", 2, 1)
+    mine = tree_sum(
+        [
+            total[:quarter].astype(f32),
+            from1[:quarter].astype(f32),
+            from2.astype(f32),
+            from3[3 * halo :].astype(f32),
+        ]
+    ).astype(bf16)
+    far = jnp.where((index == 3) | (index == 4), from3[: 3 * halo], from1[quarter:])
+    far = jnp.where((index == 0) | (index == 7), 0.0, far.astype(f32))
+    strips = halo_own + near + far
+    low, high = strips[:halo].astype(bf16), strips[2 * halo :].astype(bf16)
+    along3 = swap(jnp.concatenate([even_pick("gy", low, high), mine]), "gy", 1, 3)
+    along2 = swap(mine, "gy", 1, 2)
+    along1 = swap(jnp.concatenate([even_pick("gy", high, low), mine]), "gy", 1, 1)
+    mine = tree_sum(
+        [
+            mine.astype(f32),
+            along1[halo:].astype(f32),
+            along2.astype(f32),
+            along3[halo:].astype(f32),
+        ]
+    ).astype(bf16)
+    last_far = jnp.where((row == 0) | (row == 3), bf16(0), along3[:halo])
+    pair = jnp.concatenate([mine, swap(mine, "gx", 1, 1)])
+    parts = [pair] + [None] * 3
+    for mask in (3, 2, 1):
+        parts[mask] = swap(pair, "gx", 2, mask)
+    return parts, strips, last_far, along1[:halo]
+
+
+def sum_staged(send, keep, halo_own, halo):
+    f32, bf16 = jnp.float32, jnp.bfloat16
+    width = send.shape[1]
+    quarter = (send.shape[0] - 6 * halo) // 4
+    slots = slot_rows(quarter, halo)
+
+    def joined_slots(values):
+        return jnp.concatenate([values[spot : spot + quarter] for spot in slots])
+
+    far = send[2 * quarter : 2 * quarter + 3 * halo]
+    near = send[4 * quarter + 3 * halo :]
+    back_far, back_near = pair_exchange(far, near, "gx")
+    strips = halo_own + back_far.astype(f32) + back_near.astype(f32)
+    low, high = strips[:halo].astype(bf16), strips[2 * halo :].astype(bf16)
+    last_far, last_near = pair_exchange(
+        even_pick("gy", low, high), even_pick("gy", high, low), "gy"
+    )
+    index = lax.axis_index("gx")
+    got = swap(joined_slots(send), "gx", 1, 1)
+    total = (joined_slots(keep) + got.astype(f32)).astype(bf16)
+    split = stages(lax.axis_size("gx"))[1:]
+    for stride, factor in split:
+        part = (index // stride) % factor
+        height = total.shape[0] // factor
+        mine = lax.dynamic_slice_in_dim(total, part * height, height, 0).astype(f32)
+        for mask in range(factor - 1, 0, -1):
+            piece = lax.dynamic_slice_in_dim(total, (part ^ mask) * height, height, 0)
+            mine = mine + swap(piece, "gx", stride, mask).astype(f32)
+        total = mine.astype(bf16)
+    total = tree_sum(
+        [total.astype(f32)]
+        + [swap(total, "gy", 1, mask).astype(f32) for mask in range(1, lax.axis_size("gy"))]
+    ).astype(bf16)
+    for stride, factor in reversed(split):
+        part = (index // stride) % factor
+        height = total.shape[0]
+        joined = jnp.zeros((factor * height, width), bf16)
+        joined = lax.dynamic_update_slice_in_dim(joined, total, part * height, 0)
+        for mask in range(factor - 1, 0, -1):
+            piece = swap(total, "gx", stride, mask)
+            joined = lax.dynamic_update_slice_in_dim(joined, piece, (part ^ mask) * height, 0)
+        total = joined
+    other = swap(total, "gx", 1, 1)
+    parts = [
+        jnp.concatenate([half[m * quarter : (m + 1) * quarter] for half in (total, other)])
+        for m in range(4)
+    ]
+    return parts, strips, last_far, last_near
 
 
 def per_device(
@@ -716,61 +860,13 @@
     ring_far, ring_near = pair_exchange(ring, ring, "gy")
     unit = 16 * lax.axis_size("gx")
     grad_rows = -(-(weights.shape[0] * width + vectors.shape[0]) // unit) * unit
-    (
-        nodes_out,
-        edges_out,
-        edges_in_grad,
-        node_part,
-        halo_far,
-        halo_near,
-        halo_own,
-        grads_send,
-        grads_keep,
-    ) = layer_call(
-        halo, grad_rows, counts, neighbours, edge_mask, node_latents, ring, ring_far, ring_near,
-        node_cotangent, vectors, weights, edge_latents, edge_cotangent,
-    )
-    index = lax.axis_index("gx")
-    got = lax.ppermute(grads_send, "gx", partners("gx", 1, 1))
-    total = (grads_keep + got.astype(f32)).astype(bf16)
-    split = stages(lax.axis_size("gx"))[1:]
-    for stride, factor in split:
-        part = (index // stride) % factor
-        height = total.shape[0] // factor
-        mine = lax.dynamic_slice_in_dim(total, part * height, height, 0).astype(f32)
-        for mask in range(factor - 1, 0, -1):
-            piece = lax.dynamic_slice_in_dim(total, (part ^ mask) * height, height, 0)
-            mine = mine + lax.ppermute(piece, "gx", partners("gx", stride, mask)).astype(f32)
-        total = mine.astype(bf16)
-    total, halo_far, halo_near = lax.optimization_barrier((total, halo_far, halo_near))
-    back_far, back_near = pair_exchange(halo_far, halo_near, "gx")
-    terms = [total.astype(f32)] + [
-        lax.ppermute(total, "gy", partners("gy", 1, mask)).astype(f32)
-        for mask in range(1, lax.axis_size("gy"))
-    ]
-    while len(terms) > 1:
-        terms = [terms[i] + terms[i + 1] for i in range(0, len(terms), 2)]
-    total = terms[0].astype(bf16)
-    strips = back_far.astype(f32) + back_near.astype(f32)
-    strips = strips + jnp.concatenate(
-        [halo_own[:halo], jnp.zeros((halo, width), bf16), halo_own[halo:]], axis=0
-    ).astype(f32)
-    even_y = lax.axis_index("gy") % 2 == 0
-    low_y, high_y = strips[:halo].astype(bf16), strips[2 * halo :].astype(bf16)
-    total, low_y, high_y = lax.optimization_barrier((total, low_y, high_y))
-    last_far, last_near = pair_exchange(
-        jnp.where(even_y, low_y, high_y), jnp.where(even_y, high_y, low_y), "gy"
-    )
-    for stride, factor in reversed(split):
-        part = (index // stride) % factor
-        height = total.shape[0]
-        joined = jnp.zeros((factor * height, width), bf16)
-        joined = lax.dynamic_update_slice_in_dim(joined, total, part * height, 0)
-        for mask in range(factor - 1, 0, -1):
-            piece = lax.ppermute(total, "gx", partners("gx", stride, mask))
-            joined = lax.dynamic_update_slice_in_dim(joined, piece, (part ^ mask) * height, 0)
-        total = joined
-    other = lax.ppermute(total, "gx", partners("gx", 1, 1))
+    relayed = lax.axis_size("gx") == 8 and lax.axis_size("gy") == 4
+    nodes_out, edges_out, edges_in_grad, node_part, halo_own, send, keep = layer_call(
+        halo, relayed, grad_rows, counts, neighbours, edge_mask, node_latents, ring, ring_far,
+        ring_near, node_cotangent, vectors, weights, edge_latents, edge_cotangent,
+    )
+    sums = sum_relayed if relayed else sum_staged
+    parts, strips, last_far, last_near = sums(send, keep, halo_own.astype(f32), halo)
     boundary_grad = strips[halo : 2 * halo] + last_far.astype(f32) + last_near.astype(f32)
     returned = lax.dot_general(
         boundary_pick.astype(f32),
@@ -781,7 +877,7 @@
     )
     nodes_in_grad = (node_part + returned).astype(bf16)
     updated = update_call(
-        total, other, weights, vectors, weights_m, vectors_m, weights_v, vectors_v, weights_ema,
+        relayed, parts, weights, vectors, weights_m, vectors_m, weights_v, vectors_v, weights_ema,
         vectors_ema,
     )
     return (

time: 86.8 us -> 80.5 us (0.927)
  starting transfers between devices: 52.1 us -> 40.2 us
  waiting for transfers between devices: 7.44 us -> 14.9 us
  Pallas kernels: 19.8 us -> 18.7 us
  local copies, waits for them, and re-layouts: 1.6 us -> 0.69 us
    ppermute x11, waiting for transfers between devices: 3.79 us -> 13.9 us  [swap(): return lax.ppermute(values, axis, partners(axis, stride, mask))]
    ppermute x8 -> x4, starting transfers between devices: 13.7 us -> 4.81 us  [pair_exchange(): return (lax.ppermute(to_far, axis, far), lax.ppermute(to_near, axis, near))]
    ppermute x11, starting transfers between devices: 38.4 us -> 35.4 us  [swap(): return lax.ppermute(values, axis, partners(axis, stride, mask))]
    ppermute x8 -> x4, waiting for transfers between devices: 3.65 us -> 0.95 us  [pair_exchange(): return (lax.ppermute(to_far, axis, far), lax.ppermute(to_near, axis, near))]
    pallas_call x2, Pallas kernels: 19.8 us -> 18.7 us  [the longest x1 16.7 us: layer_call(): pl.pallas_call(functools.partial(layer_kernel, halo, relayed), out_shape=...]
  transfers between devices with their start and end apart: 19 -> 15, of which waited for: 7 -> 10; matrix products, arithmetic and copies ran while one was open for 3% -> 3% of each run, Pallas kernels for 0% -> 0%
where the time goes in v2:
time: 80.5 us; the launch traced here: 80.9 us
  starting transfers between devices  40.2 us (50%)
  Pallas kernels  18.7 us (23%)
  waiting for transfers between devices  14.9 us (19%)
  other arithmetic  3.53 us (4%)
  between operations  1.51 us (2%)
  matrix products  1.41 us (2%)
    ppermute x11, starting transfers between devices, swap(): return lax.ppermute(values, axis, partners(axis, stride, mask))  35.4 us
    pallas_call x1, Pallas kernels, layer_call(): pl.pallas_call(functools.partial(layer_kernel, halo, relayed), out_shape=...  16.7 us
    ppermute x11, waiting for transfers between devices, swap(): return lax.ppermute(values, axis, partners(axis, stride, mask))  13.9 us
    ppermute x4, starting transfers between devices, pair_exchange(): return (lax.ppermute(to_far, axis, far), lax.ppermute(to_near, axis, near))  4.81 us
    pallas_call x1, Pallas kernels, update_call(): pl.pallas_call(functools.partial(update_kernel, relayed), out_shape=tuple...  1.91 us
  transfers between devices with their start and end apart: 15, of which 10 were waited for; matrix products, arithmetic and copies ran while one was open for 3% of the time, Pallas kernels for 0%

profile of v2, /device:TPU:0, one launch (start us, length us, event | category | flops | bytes accessed | tf_op | source)
XLA Modules:
  0.0 80.9 jit_solution(18389672075392644118)
XLA Ops:
  0.6 1.0 %convolution_convert_fusion = bf16[64,128]{1,0:T(8,128)(2,1)S(1)} fusion(bf16[256,128]{1,0:T(8,128)(2,1)} %latents_ref.1, s32[64]{0:T(128)} %bitcast.13), kind=kOutput, calls=%fused_computation | convolution fusion | flops 4218880 | bytes 82176 | tf_op jit(solution)/shard_map/dot_general | solution.py:857
  2.2 0.7 collective-permute-start
  3.1 3.0 %collective-permute-start.3 = (bf16[192,128]{1,0:T(8,128)(2,1)S(1)}, bf16[192,128]{1,0:T(8,128)(2,1)S(1)}, u32[]{:S(2)}, u32[]{:S(2)}) collective-permute-start(bf16[192,128]{1,0:T(8,128)(2,1)S(1)} %pad_maximum_fusion.3.ring_ref), channel_id=1, source_target_pairs={{0,1},{1,0},{2,3},{3,2},{4,5},{5,4},{6,7},{7,6},{8,9},{9,8},{10,11... | collective-permute-start | bytes 147464 | tf_op jit(solution)/shard_map/ppermute | solution.py:722
  6.1 0.7 collective-permute-start.2
  7.4 0.8 collective-permute-done.3.ring_near_ref
  8.8 16.7 %edge_layer.1 = (bf16[256,128]{1,0:T(8,128)(2,1)}, bf16[1024,16,128]{2,1,0:T(8,128)(2,1)}, bf16[1024,16,128]{2,1,0:T(8,128)(2,1)}, f32[256,128]{1,0:T(8,128)}, b...) custom-call(s32[1]{0:T(128)S(6)} %copy.31.count_ref, s32[64,256]{1,0:T(8,128)} %bitcast.11, ...), custom_call_target="tpu_custom_call" | custom-call | tf_op jit(solution)/shard_map/edge_layer/pallas_call | solution.py:554
  25.6 3.5 %collective-permute-start.4 = (bf16[1024,128]{1,0:T(8,128)(2,1)}, bf16[1024,128]{1,0:T(8,128)(2,1)S(1)}, u32[]{:S(2)}, u32[]{:S(2)}) collective-permute-start(bf16[1024,128]{1,0:T(8,128)(2,1)} %get-tuple-element.37), channel_id=1, source_target_pairs={{0,4},{4,0},{8,12},{12,8},{16,20},{20,16},{24,28},{28,24},{1,5},{5... | collective-permute-start | bytes 786440 | tf_op jit(solution)/shard_map/ppermute | solution.py:734
  29.1 1.4 %collective-permute-done.4 = bf16[1024,128]{1,0:T(8,128)(2,1)S(1)} collective-permute-done((bf16[1024,128]{1,0:T(8,128)(2,1)}, bf16[1024,128]{1,0:T(8,128)(2,1)S(1)}, u32[]{:S(2)}, u32[]{:S(2)}) %collective-permute-start.4) | collective-permute-done | bytes 262176 | tf_op jit(solution)/shard_map/ppermute | solution.py:734
  30.5 1.1 %add_convert_fusion = bf16[832,128]{1,0:T(8,128)(2,1)S(1)} fusion(f32[832,128]{1,0:T(8,128)} %get-tuple-element.38, bf16[1024,128]{1,0:T(8,128)(2,1)S(1)} %collective-permute-done.4), kind=kLoop, calls=%fused_computation.1 | loop fusion | flops 319488 | bytes 851968 | tf_op jit(solution)/shard_map/convert_element_type | solution.py:750
  31.5 8.0 %collective-permute-start.5 = (bf16[352,128]{1,0:T(8,128)(2,1)S(1)}, bf16[352,128]{1,0:T(8,128)(2,1)S(1)}, u32[]{:S(2)}, u32[]{:S(2)}) collective-permute-start(bf16[352,128]{1,0:T(8,128)(2,1)S(1)} %get-tuple-element.53), channel_id=1, source_target_pairs={{0,24},{4,28},{8,16},{12,20},{16,8},{20,12},{24,0},{28,4},{1,25},{... | collective-permute-start | bytes 270344 | tf_op jit(solution)/shard_map/ppermute | solution.py:734
  39.6 0.6 collective-permute-start.7
  40.2 2.8 %collective-permute-done.5 = bf16[352,128]{1,0:T(8,128)(2,1)S(1)} collective-permute-done((bf16[352,128]{1,0:T(8,128)(2,1)S(1)}, bf16[352,128]{1,0:T(8,128)(2,1)S(1)}, u32[]{:S(2)}, u32[]{:S(2)}) %collective-permute-start.5) | collective-permute-done | bytes 90144 | tf_op jit(solution)/shard_map/ppermute | solution.py:734
  43.0 1.2 %collective-permute-done.6 = bf16[352,128]{1,0:T(8,128)(2,1)S(1)} collective-permute-done((bf16[352,128]{1,0:T(8,128)(2,1)S(1)}, bf16[352,128]{1,0:T(8,128)(2,1)S(1)}, u32[]{:S(2)}, u32[]{:S(2)}) %collective-permute-start.6) | collective-permute-done | bytes 90144 | tf_op jit(solution)/shard_map/ppermute | solution.py:734
  44.2 0.8 %fusion.11 = (bf16[192,128]{1,0:T(8,128)(2,1)S(1)}, f32[192,128]{1,0:T(8,128)S(1)}) fusion(bf16[352,128]{1,0:T(8,128)(2,1)S(1)} %collective-permute-done.6, bf16[352,128]{1,0:T(8,128)(2,1)S(1)} %collective-permute-done.5, pred[]{:T(512)S(6)} %or.10, pred[]{:T(512)S(6)} %or.9, bf16[1024,128]{1,0:T(8,128)(2,1)S(1)} %collective-permute-done.4, ...), kind=kLoop, calls=%fused_computation.26 | loop fusion | flops 196608 | bytes 344066 | tf_op jit(solution)/shard_map/convert.1
  45.1 13.7 %collective-permute-start.8 = (bf16[224,128]{1,0:T(8,128)(2,1)S(1)}, bf16[224,128]{1,0:T(8,128)(2,1)S(1)}, u32[]{:S(2)}, u32[]{:S(2)}) collective-permute-start(bf16[224,128]{1,0:T(8,128)(2,1)S(1)} %get-tuple-element.57), channel_id=1, source_target_pairs={{0,3},{1,2},{2,1},{3,0},{4,7},{5,6},{6,5},{7,4},{8,11},{9,10},{10,... | collective-permute-start | bytes 172040 | tf_op jit(solution)/shard_map/ppermute | solution.py:734
  58.8 5.9 %collective-permute-start.9 = (bf16[224,128]{1,0:T(8,128)(2,1)S(1)}, bf16[224,128]{1,0:T(8,128)(2,1)S(1)}, u32[]{:S(2)}, u32[]{:S(2)}) collective-permute-start(bf16[224,128]{1,0:T(8,128)(2,1)S(1)} %get-tuple-element.58), channel_id=1, source_target_pairs={{0,1},{1,0},{2,3},{3,2},{4,5},{5,4},{6,7},{7,6},{8,9},{9,8},{10,11... | collective-permute-start | bytes 172040 | tf_op jit(solution)/shard_map/ppermute | solution.py:734
  64.7 4.9 %collective-permute-done.10 = bf16[160,128]{1,0:T(8,128)(2,1)S(1)} collective-permute-done((bf16[160,128]{1,0:T(8,128)(2,1)S(1)}, bf16[160,128]{1,0:T(8,128)(2,1)S(1)}, u32[]{:S(2)}, u32[]{:S(2)}) %collective-permute-start.10) | collective-permute-done | bytes 40992 | tf_op jit(solution)/shard_map/ppermute | solution.py:734
  70.1 0.8 %collective-permute-done.11 = bf16[160,128]{1,0:T(8,128)(2,1)S(1)} collective-permute-done((bf16[160,128]{1,0:T(8,128)(2,1)S(1)}, bf16[160,128]{1,0:T(8,128)(2,1)S(1)}, u32[]{:S(2)}, u32[]{:S(2)}) %collective-permute-start.11) | collective-permute-done | bytes 40992 | tf_op jit(solution)/shard_map/ppermute | solution.py:734
  70.9 1.8 %collective-permute-start.14 = (bf16[320,128]{1,0:T(8,128)(2,1)S(1)}, bf16[320,128]{1,0:T(8,128)(2,1)S(1)}, u32[]{:S(2)}, u32[]{:S(2)}) collective-permute-start(bf16[320,128]{1,0:T(8,128)(2,1)S(1)} %pad_maximum_fusion.part0_ref), channel_id=1, source_target_pairs={{0,24},{4,28},{8,16},{12,20},{16,8},{20,12},{24,0},{28,4},{1,25},{... | collective-permute-start | bytes 245768 | tf_op jit(solution)/shard_map/ppermute | solution.py:734
  72.8 1.7 %collective-permute-start.13 = (bf16[320,128]{1,0:T(8,128)(2,1)S(1)}, bf16[320,128]{1,0:T(8,128)(2,1)S(1)}, u32[]{:S(2)}, u32[]{:S(2)}) collective-permute-start(bf16[320,128]{1,0:T(8,128)(2,1)S(1)} %pad_maximum_fusion.part0_ref), channel_id=1, source_target_pairs={{0,16},{4,20},{8,24},{12,28},{16,0},{20,4},{24,8},{28,12},{1,17},{... | collective-permute-start | bytes 245768 | tf_op jit(solution)/shard_map/ppermute | solution.py:734
  74.5 1.6 %add_convert_fusion.1 = bf16[256,128]{1,0:T(8,128)(2,1)} fusion(f32[256,128]{1,0:T(8,128)} %get-tuple-element.35, f32[256,128]{1,0:T(8,128)S(1)} %fusion), kind=kLoop, calls=%fused_computation.2 | loop fusion | flops 65536 | bytes 327680 | tf_op jit(solution)/shard_map/convert_element_type | solution.py:878
  76.4 1.7 %collective-permute-done.13.part2_ref = bf16[320,128]{1,0:T(8,128)(2,1)S(1)} collective-permute-done((bf16[320,128]{1,0:T(8,128)(2,1)S(1)}, bf16[320,128]{1,0:T(8,128)(2,1)S(1)}, u32[]{:S(2)}, u32[]{:S(2)}) %collective-permute-start.13) | collective-permute-done | bytes 81952 | tf_op jit(solution)/shard_map/ppermute | solution.py:734
  78.1 0.8 collective-permute-done.12.part1_ref
  79.0 1.9 %update.1 = (f32[1,1]{1,0:T(1,128)}, f32[9,128,128]{2,1,0:T(8,128)}, f32[10,128]{1,0:T(8,128)}, f32[9,128,128]{2,1,0:T(8,128)}, f32[10,128]{1,0:T(8,128)}, /*ind...) custom-call(bf16[320,128]{1,0:T(8,128)(2,1)S(1)} %pad_maximum_fusion, ...), custom_call_target="tpu_custom_call" | custom-call | tf_op jit(solution)/shard_map/update/pallas_call | solution.py:708
  (45 shorter events, 2.4 us)
Async XLA Ops:
  1.7 1.4 %collective-permute-start.1 = (bf16[64,128]{1,0:T(8,128)(2,1)S(1)}, bf16[64,128]{1,0:T(8,128)(2,1)S(1)}, u32[]{:S(2)}, u32[]{:S(2)}) collective-permute-start(bf16[64,128]{1,0:T(8,128)(2,1)S(1)} %convolution_convert_fusion), channel_id=1, source_target_pairs={{0,4},{4,0},{8,12},{12,8},{16,20},{20,16},{24,28},{28,24},{1,5},{5... | collective-permute-start | bytes 49160 | tf_op jit(solution)/shard_map/ppermute | solution.py:722
  2.2 0.8 %collective-permute-start = (bf16[64,128]{1,0:T(8,128)(2,1)S(1)}, bf16[64,128]{1,0:T(8,128)(2,1)S(1)}, u32[]{:S(2)}, u32[]{:S(2)}) collective-permute-start(bf16[64,128]{1,0:T(8,128)(2,1)S(1)} %convolution_convert_fusion), channel_id=1, source_target_pairs={{4,8},{12,16},{20,24},{8,4},{16,12},{24,20},{5,9},{13,17},{21,25},... | collective-permute-start | bytes 49160 | tf_op jit(solution)/shard_map/ppermute | solution.py:722
  3.1 5.1 %collective-permute-start.3 = (bf16[192,128]{1,0:T(8,128)(2,1)S(1)}, bf16[192,128]{1,0:T(8,128)(2,1)S(1)}, u32[]{:S(2)}, u32[]{:S(2)}) collective-permute-start(bf16[192,128]{1,0:T(8,128)(2,1)S(1)} %pad_maximum_fusion.3.ring_ref), channel_id=1, source_target_pairs={{0,1},{1,0},{2,3},{3,2},{4,5},{5,4},{6,7},{7,6},{8,9},{9,8},{10,11... | collective-permute-start | bytes 147464 | tf_op jit(solution)/shard_map/ppermute | solution.py:722
  6.1 2.1 %collective-permute-start.2 = (bf16[192,128]{1,0:T(8,128)(2,1)S(1)}, bf16[192,128]{1,0:T(8,128)(2,1)S(1)}, u32[]{:S(2)}, u32[]{:S(2)}) collective-permute-start(bf16[192,128]{1,0:T(8,128)(2,1)S(1)} %pad_maximum_fusion.3.ring_ref), channel_id=1, source_target_pairs={{1,2},{2,1},{5,6},{6,5},{9,10},{10,9},{13,14},{14,13},{17,18},{18,... | collective-permute-start | bytes 147464 | tf_op jit(solution)/shard_map/ppermute | solution.py:722
  8.8 61.0 %copy-start.11 = (s32[1,64]{1,0:T(1,128)S(1)}, s32[1,64]{1,0:T(1,128)}, u32[]{:S(2)}) copy-start(s32[1,64]{1,0:T(1,128)} %param.22) | copy-start | bytes 772
  8.8 70.1 %copy-start = (f32[9,128,128]{2,1,0:T(8,128)S(1)}, f32[9,128,128]{2,1,0:T(8,128)}, u32[]{:S(2)}) copy-start(f32[9,128,128]{2,1,0:T(8,128)} %weights_ref.1) | copy-start | bytes 1769476
  8.8 70.1 %copy-start.1 = (f32[9,128,128]{2,1,0:T(8,128)S(1)}, f32[9,128,128]{2,1,0:T(8,128)}, u32[]{:S(2)}) copy-start(f32[9,128,128]{2,1,0:T(8,128)} %weights_m_ref.1) | copy-start | bytes 1769476
  8.8 70.1 %copy-start.2 = (f32[9,128,128]{2,1,0:T(8,128)S(1)}, f32[9,128,128]{2,1,0:T(8,128)}, u32[]{:S(2)}) copy-start(f32[9,128,128]{2,1,0:T(8,128)} %weights_v_ref.1) | copy-start | bytes 1769476
  8.8 70.1 %copy-start.3 = (f32[9,128,128]{2,1,0:T(8,128)S(1)}, f32[9,128,128]{2,1,0:T(8,128)}, u32[]{:S(2)}) copy-start(f32[9,128,128]{2,1,0:T(8,128)} %weights_ema_ref.1) | copy-start | bytes 1769476
  8.8 70.1 %copy-start.4 = (f32[10,128]{1,0:T(8,128)S(1)}, f32[10,128]{1,0:T(8,128)}, u32[]{:S(2)}) copy-start(f32[10,128]{1,0:T(8,128)} %vectors_ref.3) | copy-start | bytes 15364
  8.8 70.1 %copy-start.5 = (f32[10,128]{1,0:T(8,128)S(1)}, f32[10,128]{1,0:T(8,128)}, u32[]{:S(2)}) copy-start(f32[10,128]{1,0:T(8,128)} %vectors_m_ref.1) | copy-start | bytes 15364
  8.8 70.1 %copy-start.6 = (f32[10,128]{1,0:T(8,128)S(1)}, f32[10,128]{1,0:T(8,128)}, u32[]{:S(2)}) copy-start(f32[10,128]{1,0:T(8,128)} %vectors_v_ref.1) | copy-start | bytes 15364
  8.8 70.1 %copy-start.7 = (f32[10,128]{1,0:T(8,128)S(1)}, f32[10,128]{1,0:T(8,128)}, u32[]{:S(2)}) copy-start(f32[10,128]{1,0:T(8,128)} %vectors_ema_ref.1) | copy-start | bytes 15364
  25.6 4.9 %collective-permute-start.4 = (bf16[1024,128]{1,0:T(8,128)(2,1)}, bf16[1024,128]{1,0:T(8,128)(2,1)S(1)}, u32[]{:S(2)}, u32[]{:S(2)}) collective-permute-start(bf16[1024,128]{1,0:T(8,128)(2,1)} %get-tuple-element.37), channel_id=1, source_target_pairs={{0,4},{4,0},{8,12},{12,8},{16,20},{20,16},{24,28},{28,24},{1,5},{5... | collective-permute-start | bytes 786440 | tf_op jit(solution)/shard_map/ppermute | solution.py:734
  31.5 11.4 %collective-permute-start.5 = (bf16[352,128]{1,0:T(8,128)(2,1)S(1)}, bf16[352,128]{1,0:T(8,128)(2,1)S(1)}, u32[]{:S(2)}, u32[]{:S(2)}) collective-permute-start(bf16[352,128]{1,0:T(8,128)(2,1)S(1)} %get-tuple-element.53), channel_id=1, source_target_pairs={{0,24},{4,28},{8,16},{12,20},{16,8},{20,12},{24,0},{28,4},{1,25},{... | collective-permute-start | bytes 270344 | tf_op jit(solution)/shard_map/ppermute | solution.py:734
  39.6 4.6 %collective-permute-start.6 = (bf16[352,128]{1,0:T(8,128)(2,1)S(1)}, bf16[352,128]{1,0:T(8,128)(2,1)S(1)}, u32[]{:S(2)}, u32[]{:S(2)}) collective-permute-start(bf16[352,128]{1,0:T(8,128)(2,1)S(1)} %get-tuple-element.54), channel_id=1, source_target_pairs={{0,8},{4,12},{8,0},{12,4},{16,24},{20,28},{24,16},{28,20},{1,9},{5... | collective-permute-start | bytes 270344 | tf_op jit(solution)/shard_map/ppermute | solution.py:734
  39.6 5.4 %collective-permute-start.7 = (bf16[160,128]{1,0:T(8,128)(2,1)S(1)}, bf16[160,128]{1,0:T(8,128)(2,1)S(1)}, u32[]{:S(2)}, u32[]{:S(2)}) collective-permute-start(bf16[160,128]{1,0:T(8,128)(2,1)S(1)} %slice.81), channel_id=1, source_target_pairs={{0,16},{4,20},{8,24},{12,28},{16,0},{20,4},{24,8},{28,12},{1,17},{... | collective-permute-start | bytes 122888 | tf_op jit(solution)/shard_map/ppermute | solution.py:734
  45.1 24.5 %collective-permute-start.8 = (bf16[224,128]{1,0:T(8,128)(2,1)S(1)}, bf16[224,128]{1,0:T(8,128)(2,1)S(1)}, u32[]{:S(2)}, u32[]{:S(2)}) collective-permute-start(bf16[224,128]{1,0:T(8,128)(2,1)S(1)} %get-tuple-element.57), channel_id=1, source_target_pairs={{0,3},{1,2},{2,1},{3,0},{4,7},{5,6},{6,5},{7,4},{8,11},{9,10},{10,... | collective-permute-start | bytes 172040 | tf_op jit(solution)/shard_map/ppermute | solution.py:734
  58.8 10.8 %collective-permute-start.9 = (bf16[224,128]{1,0:T(8,128)(2,1)S(1)}, bf16[224,128]{1,0:T(8,128)(2,1)S(1)}, u32[]{:S(2)}, u32[]{:S(2)}) collective-permute-start(bf16[224,128]{1,0:T(8,128)(2,1)S(1)} %get-tuple-element.58), channel_id=1, source_target_pairs={{0,1},{1,0},{2,3},{3,2},{4,5},{5,4},{6,7},{7,6},{8,9},{9,8},{10,11... | collective-permute-start | bytes 172040 | tf_op jit(solution)/shard_map/ppermute | solution.py:734
  64.7 4.9 %collective-permute-start.10 = (bf16[160,128]{1,0:T(8,128)(2,1)S(1)}, bf16[160,128]{1,0:T(8,128)(2,1)S(1)}, u32[]{:S(2)}, u32[]{:S(2)}) collective-permute-start(bf16[160,128]{1,0:T(8,128)(2,1)S(1)} %add_convert_fusion.3), channel_id=1, source_target_pairs={{0,2},{1,3},{2,0},{3,1},{4,6},{5,7},{6,4},{7,5},{8,10},{9,11},{10,... | collective-permute-start | bytes 122888 | tf_op jit(solution)/shard_map/ppermute | solution.py:734
  69.6 1.3 %collective-permute-start.11 = (bf16[160,128]{1,0:T(8,128)(2,1)S(1)}, bf16[160,128]{1,0:T(8,128)(2,1)S(1)}, u32[]{:S(2)}, u32[]{:S(2)}) collective-permute-start(bf16[160,128]{1,0:T(8,128)(2,1)S(1)} %add_convert_fusion.2), channel_id=1, source_target_pairs={{0,4},{4,0},{8,12},{12,8},{16,20},{20,16},{24,28},{28,24},{1,5},{5... | collective-permute-start | bytes 122888 | tf_op jit(solution)/shard_map/ppermute | solution.py:734
  70.9 5.5 %collective-permute-start.14 = (bf16[320,128]{1,0:T(8,128)(2,1)S(1)}, bf16[320,128]{1,0:T(8,128)(2,1)S(1)}, u32[]{:S(2)}, u32[]{:S(2)}) collective-permute-start(bf16[320,128]{1,0:T(8,128)(2,1)S(1)} %pad_maximum_fusion.part0_ref), channel_id=1, source_target_pairs={{0,24},{4,28},{8,16},{12,20},{16,8},{20,12},{24,0},{28,4},{1,25},{... | collective-permute-start | bytes 245768 | tf_op jit(solution)/shard_map/ppermute | solution.py:734
  72.8 5.3 %collective-permute-start.13 = (bf16[320,128]{1,0:T(8,128)(2,1)S(1)}, bf16[320,128]{1,0:T(8,128)(2,1)S(1)}, u32[]{:S(2)}, u32[]{:S(2)}) collective-permute-start(bf16[320,128]{1,0:T(8,128)(2,1)S(1)} %pad_maximum_fusion.part0_ref), channel_id=1, source_target_pairs={{0,16},{4,20},{8,24},{12,28},{16,0},{20,4},{24,8},{28,12},{1,17},{... | collective-permute-start | bytes 245768 | tf_op jit(solution)/shard_map/ppermute | solution.py:734
  74.5 4.4 %collective-permute-start.12 = (bf16[320,128]{1,0:T(8,128)(2,1)S(1)}, bf16[320,128]{1,0:T(8,128)(2,1)S(1)}, u32[]{:S(2)}, u32[]{:S(2)}) collective-permute-start(bf16[320,128]{1,0:T(8,128)(2,1)S(1)} %pad_maximum_fusion.part0_ref), channel_id=1, source_target_pairs={{0,8},{4,12},{8,0},{12,4},{16,24},{20,28},{24,16},{28,20},{1,9},{5... | collective-permute-start | bytes 245768 | tf_op jit(solution)/shard_map/ppermute | solution.py:734
  (3 other events, 6.3 us)
